TPU v7x, 32 devices: a whole 2x2x4 slice. The times are simulated.
32 devices in a mesh: gx: 4 (over y, core), gy: 4 (over z), gz: 2 (over x).
Axes of the slice: x: 2, y: 2, z: 4, core: 2. Of those that a mesh axis runs over, the one named last changes fastest.
Arguments:
- positions: float32 [3, 4096], P(None, ('gx', 'gy', 'gz')), may hold values from -8 to 8
- atom_features: float32 [4096, 128], P(('gx', 'gy', 'gz')), may hold values from -6 to 6
- send_face: int32 [32, 6, 32], P(('gx', 'gy', 'gz')), may hold values from 0 to 127
- send_edge: int32 [32, 12, 8], P(('gx', 'gy', 'gz')), may hold values from 0 to 127
- send_corner: int32 [32, 8, 2], P(('gx', 'gy', 'gz')), may hold values from 0 to 127
- centre: int32 [196608], P(('gx', 'gy', 'gz')), may hold values from 0 to 127
- other: int32 [196608], P(('gx', 'gy', 'gz')), may hold values from 0 to 431
- edge_count: int32 [32], P(('gx', 'gy', 'gz')), may hold values from 1536 to 6144, as said below
- w_proj_a: float32 [128, 128], replicated, may hold values from -0.5 to 0.5
- w_proj_b: float32 [128, 128], replicated, may hold values from -0.5 to 0.5
- w_radial: float32 [8, 128], replicated, may hold values from -2 to 2
- w_first: bfloat16 [128, 128], replicated, may hold values from -0.5 to 0.5
- w_env: bfloat16 [128, 128], replicated, may hold values from -0.5 to 0.5
- w_value: bfloat16 [128, 128], replicated, may hold values from -0.5 to 0.5
- w_second: bfloat16 [256, 128], replicated, may hold values from -0.375 to 0.375
- w_out: bfloat16 [128], replicated, may hold values from -0.5 to 0.5
Outputs:
- forces: float32 [3, 4096], P(None, ('gx', 'gy', 'gz'))
- atom_energy: float32 [4096], P(('gx', 'gy', 'gz'))
- feature_grad: float32 [4096, 128], P(('gx', 'gy', 'gz'))
Inputs may be any that keep to these rules, and one draw needn't show every extreme that they name: `edge_count`: some domain has exactly 6144 live edges in every draw.
All inputs are finite; a program needn't handle non-finite values.
Results may differ from a plain program's by a relative error of at most 0.035.
Values sent between devices are 32-bit elements; how exact they have to be, the bound alone decides.
No kernel may reach another device: no remote copies, remote signals or barrier semaphores. Data moves between devices by JAX's collectives and lax.ppermute only.
A program may use at most 192 MiB of HBM per device.

v0:
```python
import math

import jax
import jax.numpy as jnp
import numpy as np
from jax import lax
from jax.sharding import PartitionSpec as P


def padded(cells, sides, width):
    for axis, dim in sides:
        count = lax.axis_size(axis)
        head = lax.slice_in_dim(cells, 0, width, axis=dim)
        tail = lax.slice_in_dim(cells, cells.shape[dim] - width, cells.shape[dim], axis=dim)
        cells = jnp.concatenate(
            [
                lax.ppermute(tail, axis, [(i, (i + 1) % count) for i in range(count)]),
                cells,
                lax.ppermute(head, axis, [((i + 1) % count, i) for i in range(count)]),
            ],
            axis=dim,
        )
    return cells


def offsets_table():
    rows = []
    for a in (-1, 0, 1):
        for b in (-1, 0, 1):
            for c in (-1, 0, 1):
                if a != 0 or b != 0 or c != 0:
                    rows.append((a, b, c))
    return np.array(rows, dtype=np.int32)


def class_keys():
    groups = [[], [], []]
    index = 0
    for a in (-1, 0, 1):
        for b in (-1, 0, 1):
            for c in (-1, 0, 1):
                if a != 0 or b != 0 or c != 0:
                    groups[abs(a) + abs(b) + abs(c) - 1].append(index)
                    index = index + 1
    return [np.array(group, dtype=np.int32) for group in groups]


def harmonics(unit):
    ux, uy, uz = (unit[0], unit[1], unit[2])
    return [
        jnp.ones_like(ux),
        ux,
        uy,
        uz,
        1.732 * ux * uy,
        1.732 * uy * uz,
        1.732 * ux * uz,
        0.866 * (ux * ux - uy * uy),
        0.5 * (3.0 * uz * uz - 1.0),
    ]


def local_energy(
    pos_tab,
    proj_a,
    proj_b,
    centre,
    other,
    valid,
    w_radial,
    w_first,
    w_env,
    w_value,
    w_second,
    w_out,
):
    n_own = proj_a.shape[0]
    disp = jnp.take(pos_tab, other, axis=1) - jnp.take(pos_tab, centre, axis=1)
    dist = jnp.sqrt(jnp.sum(disp * disp, axis=0) + 0.01)
    unit = disp / dist[None, :]
    envelope = 1.0 / (1.0 + (dist / 2.0) ** 2) ** 2
    orders = jnp.arange(1, w_radial.shape[0] + 1).astype(jnp.float32)
    basis = (
        jnp.sin(orders[None, :] * (math.pi / 2.0) * dist[:, None])
        / dist[:, None]
        * envelope[:, None]
    )
    radial = jnp.dot(basis, w_radial, precision=lax.Precision.HIGHEST)
    mixed = (jnp.take(proj_a, centre, axis=0) + jnp.take(proj_b, other, axis=0) + radial).astype(
        jnp.bfloat16
    )
    first = jax.nn.silu(jnp.dot(mixed, w_first, preferred_element_type=jnp.float32)).astype(
        jnp.bfloat16
    )
    env_weight = (
        jnp.dot(first, w_env, preferred_element_type=jnp.float32) * (envelope * valid)[:, None]
    )
    value = jnp.dot(first, w_value, preferred_element_type=jnp.float32)
    total = jnp.zeros(value.shape, jnp.float32)
    for comp in harmonics(unit):
        env_m = jax.ops.segment_sum(env_weight * comp[:, None], centre, num_segments=n_own)
        total = total + comp[:, None] * jnp.take(env_m, centre, axis=0)
    scalar = (0.2 * value * total).astype(jnp.bfloat16)
    joined = jnp.concatenate([first, scalar], axis=1)
    second = jax.nn.silu(jnp.dot(joined, w_second, preferred_element_type=jnp.float32)).astype(
        jnp.bfloat16
    )
    edge_energy = jnp.dot(second, w_out, preferred_element_type=jnp.float32) * envelope * valid
    atom_energy = jax.ops.segment_sum(edge_energy, centre, num_segments=n_own)
    return (jnp.sum(edge_energy), atom_energy)


def place(items):
    blank = jnp.zeros_like(items[:1])
    return jnp.concatenate([items[:13], blank, items[13:]], axis=0).reshape(
        (3, 3, 3) + items.shape[1:]
    )


def place_back(items):
    slots = place(items).reshape((27,) + items.shape[1:])
    return slots[::-1].reshape((3, 3, 3) + items.shape[1:])


def pick(extended, flat_index):
    merged = extended.reshape((125,) + extended.shape[3:])
    return jnp.take(merged, jnp.asarray(flat_index), axis=0)


def lift(items, keys):
    full = jnp.zeros((26,) + items.shape[1:], items.dtype)
    return full.at[jnp.asarray(keys)].set(items)


def widen(items, axis, width):
    extra = width - items.shape[axis]
    pads = [(0, 0)] * items.ndim
    pads[axis] = (0, extra)
    return jnp.pad(items, pads)


def local(
    positions,
    atom_features,
    send_face,
    send_edge,
    send_corner,
    centre,
    other,
    edge_count,
    w_proj_a,
    w_proj_b,
    w_radial,
    w_first,
    w_env,
    w_value,
    w_second,
    w_out,
):
    high = lax.Precision.HIGHEST
    n_own = positions.shape[1]
    chans = atom_features.shape[1]
    keys_all = class_keys()
    lists_all = [send_face[0], send_edge[0], send_corner[0]]
    widths = [lists.shape[1] for lists in lists_all]
    widest = widths[0]
    flat_all = jnp.concatenate([lists.reshape(-1) for lists in lists_all], axis=0)
    offs = offsets_table()
    incoming = (2 - 2 * offs[:, 0]) * 25 + (2 - 2 * offs[:, 1]) * 5 + (2 - 2 * offs[:, 2])
    outgoing = (2 + 2 * offs[:, 0]) * 25 + (2 + 2 * offs[:, 1]) * 5 + (2 + 2 * offs[:, 2])
    proj_a = jnp.dot(atom_features, w_proj_a, precision=high)
    send_rows = []
    send_pos = []
    for keys, lists, width in zip(keys_all, lists_all, widths):
        flat_list = lists.reshape(-1)
        send_rows.append(
            jnp.take(atom_features, flat_list, axis=0).reshape(keys.shape[0], width, chans)
        )
        send_pos.append(
            jnp.transpose(
                jnp.take(positions, flat_list, axis=1).reshape(3, keys.shape[0], width), (1, 0, 2)
            )
        )
    recv_rows = []
    recv_pos = []
    full_rows = sum((lift(widen(r, 1, widest), k) for r, k in zip(send_rows, keys_all)))
    full_pos = sum((lift(widen(p, 2, widest), k) for p, k in zip(send_pos, keys_all)))
    ext_rows, ext_pos = (
        padded(place(full_rows), (("gx", 0), ("gy", 1), ("gz", 2)), 1),
        padded(place(full_pos), (("gx", 0), ("gy", 1), ("gz", 2)), 1),
    )
    all_rows = pick(ext_rows, incoming)
    all_pos = pick(ext_pos, incoming)
    for keys, width in zip(keys_all, widths):
        recv_rows.append(all_rows[keys][:, :width])
        recv_pos.append(all_pos[keys][:, :, :width])
    ghost_rows = jnp.concatenate([r.reshape(-1, chans) for r in recv_rows], axis=0)
    ghost_pos = jnp.concatenate(
        [jnp.transpose(p, (1, 0, 2)).reshape(3, -1) for p in recv_pos], axis=1
    )
    pos_tab = jnp.concatenate([positions, ghost_pos], axis=1)
    own_b = jnp.dot(atom_features, w_proj_b, precision=high)
    proj_tab = jnp.concatenate([own_b, jnp.dot(ghost_rows, w_proj_b, precision=high)], axis=0)
    valid = (jnp.arange(centre.shape[0]) < edge_count[0]).astype(jnp.float32)

    def energy(p, a, b):
        return local_energy(
            p, a, b, centre, other, valid, w_radial, w_first, w_env, w_value, w_second, w_out
        )

    total, pullback, atom_energy = jax.vjp(energy, pos_tab, proj_a, proj_tab, has_aux=True)
    grad_pos, grad_a, grad_b = pullback(jnp.ones((), jnp.float32))
    ghost_grad = jnp.dot(grad_b[n_own:], w_proj_b.T, precision=high)
    back_rows = []
    back_pos = []
    start = 0
    for keys, width in zip(keys_all, widths):
        count = keys.shape[0] * width
        back_rows.append(ghost_grad[start : start + count].reshape(keys.shape[0], width, chans))
        back_pos.append(
            jnp.transpose(
                grad_pos[:, n_own + start : n_own + start + count].reshape(3, keys.shape[0], width),
                (1, 0, 2),
            )
        )
        start = start + count
    got_rows = []
    got_pos = []
    full_rows = sum((lift(widen(r, 1, widest), k) for r, k in zip(back_rows, keys_all)))
    full_pos = sum((lift(widen(p, 2, widest), k) for p, k in zip(back_pos, keys_all)))
    ret_rows, ret_pos = (
        padded(place_back(full_rows), (("gx", 0), ("gy", 1), ("gz", 2)), 1),
        padded(place_back(full_pos), (("gx", 0), ("gy", 1), ("gz", 2)), 1),
    )
    all_rows = pick(ret_rows, outgoing)
    all_pos = pick(ret_pos, outgoing)
    for keys, width in zip(keys_all, widths):
        got_rows.append(all_rows[keys][:, :width])
        got_pos.append(all_pos[keys][:, :, :width])
    returned_rows = jnp.concatenate([r.reshape(-1, chans) for r in got_rows], axis=0)
    returned_pos = jnp.concatenate(
        [jnp.transpose(p, (0, 2, 1)).reshape(-1, 3) for p in got_pos], axis=0
    )
    force_sum = (
        grad_pos[:, :n_own] + jax.ops.segment_sum(returned_pos, flat_all, num_segments=n_own).T
    )
    added_rows = jax.ops.segment_sum(returned_rows, flat_all, num_segments=n_own)
    feature_grad = (
        jnp.dot(grad_a, w_proj_a.T, precision=high)
        + jnp.dot(grad_b[:n_own], w_proj_b.T, precision=high)
        + added_rows
    )
    return (-force_sum, atom_energy, feature_grad)


def solution(mesh):
    return jax.shard_map(
        local,
        mesh=mesh,
        in_specs=(
            P(None, ("gx", "gy", "gz")),
            P(("gx", "gy", "gz"), None),
            P(("gx", "gy", "gz"), None, None),
            P(("gx", "gy", "gz"), None, None),
            P(("gx", "gy", "gz"), None, None),
            P(("gx", "gy", "gz")),
            P(("gx", "gy", "gz")),
            P(("gx", "gy", "gz")),
            P(),
            P(),
            P(),
            P(),
            P(),
            P(),
            P(),
            P(),
        ),
        out_specs=(P(None, ("gx", "gy", "gz")), P(("gx", "gy", "gz")), P(("gx", "gy", "gz"), None)),
        check_vma=False,
    )
```

profile of v0, /device:TPU:0, one launch (start us, length us, event | category | flops | bytes accessed | tf_op | source)
XLA Modules:
  0.0 1532.0 jit_solution(2786530594837218440)
XLA Ops:
  42.0 16.1 %gather_fusion.30 = f32[6144,128]{1,0:T(8,128)S(1)} fusion(f32[128,128]{1,0:T(8,128)S(1)} %fusion.145, s32[6144]{0:T(1024)S(1)} %get-tuple-element.176), kind=kCustom, calls=%fused_computation.2.clone | custom fusion | bytes 6316032 | tf_op jit(solution)/shard_map/jvp(jit(_take))/gather | solution.py:89
  65.3 21.0 %gather_fusion.32 = f32[6144,3]{1,0:T(8,128)} fusion(f32[3,432]{0,1:T(8,128)S(1)} %copy.435, s32[6144]{0:T(1024)S(1)} %get-tuple-element.167), kind=kCustom, calls=%fused_computation.5.clone | custom fusion | bytes 172032 | tf_op jit(solution)/shard_map/jvp(jit(_take))/gather | solution.py:78
  89.4 21.0 %gather_fusion.29 = f32[6144,3]{1,0:T(8,128)} fusion(f32[3,432]{0,1:T(8,128)S(1)} %copy.435, s32[6144]{0:T(1024)S(1)} %copy-done.68), kind=kCustom, calls=%fused_computation.1.clone | custom fusion | bytes 172032 | tf_op jit(solution)/shard_map/jvp(jit(_take))/gather | solution.py:78
  163.1 23.2 %gather_fusion.12 = f32[6144,128]{1,0:T(8,128)} fusion(f32[432,128]{1,0:T(8,128)S(1)} %pad_maximum_fusion.22, s32[6144]{0:T(1024)} %copy-done.41), kind=kCustom, calls=%fused_computation.28 | custom fusion | bytes 6316032 | tf_op jit(solution)/shard_map/jvp(jit(_take))/gather | solution.py:89
  186.3 10.8 fusion
  208.1 33.5 %scatter_custom_fusion.7 = f32[128,128]{1,0:T(8,128)S(1)} fusion(s32[6144]{0:T(1024)} %param.46, f32[6144,128]{1,0:T(8,128)} %copy.441, f32[]{:T(128)} %constant.138.clone.1), kind=kCustom, calls=%fused_computation.300 | custom fusion | flops 786432 | bytes 66048 | tf_op jit(solution)/shard_map/jvp()/scatter-add | solution.py:101
  241.6 20.9 %gather_fusion.34 = f32[6144,128]{1,0:T(8,128)} fusion(f32[128,128]{1,0:T(8,128)S(1)} %scatter_custom_fusion.7, s32[6144]{0:T(1024)S(1)} %get-tuple-element.176), kind=kCustom, calls=%fused_computation.7.clone | custom fusion | bytes 6316032 | tf_op jit(solution)/shard_map/jvp(jit(_take))/gather | solution.py:102
  268.5 33.7 %scatter_custom_fusion.6 = f32[128,128]{1,0:T(8,128)S(1)} fusion(s32[6144]{0:T(1024)} %param.46, f32[6144,128]{1,0:T(8,128)} %copy.439, f32[]{:T(128)} %constant.138.clone.1), kind=kCustom, calls=%fused_computation.302 | custom fusion | flops 786432 | bytes 66048 | tf_op jit(solution)/shard_map/jvp()/scatter-add | solution.py:101
  302.2 20.9 %gather_fusion.33 = f32[6144,128]{1,0:T(8,128)} fusion(f32[128,128]{1,0:T(8,128)S(1)} %scatter_custom_fusion.6, s32[6144]{0:T(1024)S(1)} %get-tuple-element.176), kind=kCustom, calls=%fused_computation.6.clone | custom fusion | bytes 6316032 | tf_op jit(solution)/shard_map/jvp(jit(_take))/gather | solution.py:102
  337.0 33.4 %scatter_custom_fusion.8 = f32[128,128]{1,0:T(8,128)S(1)} fusion(s32[6144]{0:T(1024)} %param.46, f32[6144,128]{1,0:T(8,128)S(1)} %copy.443, f32[]{:T(128)} %constant.138.clone.1), kind=kCustom, calls=%fused_computation.298 | custom fusion | flops 786432 | bytes 66048 | tf_op jit(solution)/shard_map/jvp()/scatter-add | solution.py:101
  370.3 16.1 %gather_fusion.35 = f32[6144,128]{1,0:T(8,128)S(1)} fusion(f32[128,128]{1,0:T(8,128)S(1)} %scatter_custom_fusion.8, s32[6144]{0:T(1024)S(1)} %get-tuple-element.176), kind=kCustom, calls=%fused_computation.8.clone | custom fusion | bytes 6316032 | tf_op jit(solution)/shard_map/jvp(jit(_take))/gather | solution.py:102
  391.2 33.4 %scatter_custom_fusion.14 = f32[128,128]{1,0:T(8,128)S(1)} fusion(s32[6144]{0:T(1024)} %param.46, f32[6144,128]{1,0:T(8,128)S(1)} %copy.455, f32[]{:T(128)} %constant.138.clone.1), kind=kCustom, calls=%fused_computation.286 | custom fusion | flops 786432 | bytes 66048 | tf_op jit(solution)/shard_map/jvp()/scatter-add | solution.py:101
  424.6 16.1 %gather_fusion.41 = f32[6144,128]{1,0:T(8,128)S(1)} fusion(f32[128,128]{1,0:T(8,128)S(1)} %scatter_custom_fusion.14, s32[6144]{0:T(1024)S(1)} %get-tuple-element.176), kind=kCustom, calls=%fused_computation.14.clone | custom fusion | bytes 6316032 | tf_op jit(solution)/shard_map/jvp(jit(_take))/gather | solution.py:102
  445.4 33.8 %scatter_custom_fusion.13 = f32[128,128]{1,0:T(8,128)S(1)} fusion(s32[6144]{0:T(1024)} %param.46, f32[6144,128]{1,0:T(8,128)S(1)} %copy.453, f32[]{:T(128)} %constant.138.clone.1), kind=kCustom, calls=%fused_computation.288 | custom fusion | flops 786432 | bytes 66048 | tf_op jit(solution)/shard_map/jvp()/scatter-add | solution.py:101
  479.2 16.1 %gather_fusion.40 = f32[6144,128]{1,0:T(8,128)S(1)} fusion(f32[128,128]{1,0:T(8,128)S(1)} %scatter_custom_fusion.13, s32[6144]{0:T(1024)S(1)} %get-tuple-element.176), kind=kCustom, calls=%fused_computation.13.clone | custom fusion | bytes 6316032 | tf_op jit(solution)/shard_map/jvp(jit(_take))/gather | solution.py:102
  500.0 33.4 %scatter_custom_fusion.12 = f32[128,128]{1,0:T(8,128)S(1)} fusion(s32[6144]{0:T(1024)} %param.46, f32[6144,128]{1,0:T(8,128)S(1)} %copy.451, f32[]{:T(128)} %constant.138.clone.1), kind=kCustom, calls=%fused_computation.290 | custom fusion | flops 786432 | bytes 66048 | tf_op jit(solution)/shard_map/jvp()/scatter-add | solution.py:101
  533.4 16.1 %gather_fusion.39 = f32[6144,128]{1,0:T(8,128)S(1)} fusion(f32[128,128]{1,0:T(8,128)S(1)} %scatter_custom_fusion.12, s32[6144]{0:T(1024)S(1)} %get-tuple-element.176), kind=kCustom, calls=%fused_computation.12.clone | custom fusion | bytes 6316032 | tf_op jit(solution)/shard_map/jvp(jit(_take))/gather | solution.py:102
  554.2 33.4 %scatter_custom_fusion.11 = f32[128,128]{1,0:T(8,128)S(1)} fusion(s32[6144]{0:T(1024)} %param.46, f32[6144,128]{1,0:T(8,128)S(1)} %copy.449, f32[]{:T(128)} %constant.138.clone.1), kind=kCustom, calls=%fused_computation.292 | custom fusion | flops 786432 | bytes 66048 | tf_op jit(solution)/shard_map/jvp()/scatter-add | solution.py:101
  587.6 16.1 %gather_fusion.38 = f32[6144,128]{1,0:T(8,128)S(1)} fusion(f32[128,128]{1,0:T(8,128)S(1)} %scatter_custom_fusion.11, s32[6144]{0:T(1024)S(1)} %get-tuple-element.176), kind=kCustom, calls=%fused_computation.11.clone | custom fusion | bytes 6316032 | tf_op jit(solution)/shard_map/jvp(jit(_take))/gather | solution.py:102
  608.4 33.4 %scatter_custom_fusion.10 = f32[128,128]{1,0:T(8,128)S(1)} fusion(s32[6144]{0:T(1024)} %param.46, f32[6144,128]{1,0:T(8,128)S(1)} %copy.447, f32[]{:T(128)} %constant.138.clone.1), kind=kCustom, calls=%fused_computation.294 | custom fusion | flops 786432 | bytes 66048 | tf_op jit(solution)/shard_map/jvp()/scatter-add | solution.py:101
  641.8 16.1 %gather_fusion.37 = f32[6144,128]{1,0:T(8,128)S(1)} fusion(f32[128,128]{1,0:T(8,128)S(1)} %scatter_custom_fusion.10, s32[6144]{0:T(1024)S(1)} %get-tuple-element.176), kind=kCustom, calls=%fused_computation.10.clone | custom fusion | bytes 6316032 | tf_op jit(solution)/shard_map/jvp(jit(_take))/gather | solution.py:102
  662.7 33.5 %scatter_custom_fusion.9 = f32[128,128]{1,0:T(8,128)S(1)} fusion(s32[6144]{0:T(1024)} %param.46, f32[6144,128]{1,0:T(8,128)S(1)} %copy.445, f32[]{:T(128)} %constant.138.clone.1), kind=kCustom, calls=%fused_computation.296 | custom fusion | flops 786432 | bytes 66048 | tf_op jit(solution)/shard_map/jvp()/scatter-add | solution.py:101
  696.3 20.9 %gather_fusion.36 = f32[6144,128]{1,0:T(8,128)} fusion(f32[128,128]{1,0:T(8,128)S(1)} %scatter_custom_fusion.9, s32[6144]{0:T(1024)S(1)} %get-tuple-element.176), kind=kCustom, calls=%fused_computation.9.clone | custom fusion | bytes 6316032 | tf_op jit(solution)/shard_map/jvp(jit(_take))/gather | solution.py:102
  721.0 13.9 multiply_convert_fusion.1
  742.8 17.9 %broadcast_multiply_fusion.4 = (f32[6144,128]{0,1:T(8,128)}, f32[6144,128]{0,1:T(8,128)}, f32[6144,128]{0,1:T(8,128)}, f32[6144,128]{0,1:T(8,128)}, f32[6144,128...) fusion(f32[6144,128]{0,1:T(8,128)} %get-tuple-element.95, ...), kind=kLoop, calls=%fused_computation.152 | loop fusion | flops 24330240 | bytes 50706432 | tf_op jit(solution)/shard_map/transpose(jvp())/mul | solution.py:102
  774.0 33.7 %scatter_custom_fusion.17 = f32[128,128]{1,0:T(8,128)S(1)} fusion(s32[6144]{0:T(1024)} %get-tuple-element.178, f32[6144,128]{1,0:T(8,128)} %copy.463, f32[]{:T(128)} %constant.138.clone.1), kind=kCustom, calls=%fused_computation.280 | custom fusion | flops 786432 | bytes 66048 | tf_op jit(solution)/shard_map/transpose(jvp(jit(_take)))/scatter-add | solution.py:102
  807.7 16.1 %gather_fusion.15 = f32[6144,128]{1,0:T(8,128)S(1)} fusion(f32[128,128]{1,0:T(8,128)S(1)} %scatter_custom_fusion.17, s32[6144]{0:T(1024)S(1)} %copy-done.17), kind=kCustom, calls=%fused_computation.31 | custom fusion | bytes 6316032 | tf_op jit(solution)/shard_map/transpose(jvp())/gather | solution.py:101
  826.2 33.5 %scatter_custom_fusion.16 = f32[128,128]{1,0:T(8,128)S(1)} fusion(s32[6144]{0:T(1024)} %get-tuple-element.178, f32[6144,128]{1,0:T(8,128)} %copy.461, f32[]{:T(128)} %constant.138.clone.1), kind=kCustom, calls=%fused_computation.282 | custom fusion | flops 786432 | bytes 66048 | tf_op jit(solution)/shard_map/transpose(jvp(jit(_take)))/scatter-add | solution.py:102
  859.6 16.1 %gather_fusion.14 = f32[6144,128]{1,0:T(8,128)S(1)} fusion(f32[128,128]{1,0:T(8,128)S(1)} %scatter_custom_fusion.16, s32[6144]{0:T(1024)S(1)} %copy-done.17), kind=kCustom, calls=%fused_computation.30 | custom fusion | bytes 6316032 | tf_op jit(solution)/shard_map/transpose(jvp())/gather | solution.py:101
  880.5 33.4 %scatter_custom_fusion.21 = f32[128,128]{1,0:T(8,128)S(1)} fusion(s32[6144]{0:T(1024)} %get-tuple-element.178, f32[6144,128]{1,0:T(8,128)S(1)} %copy.471, f32[]{:T(128)} %constant.138.clone.1), kind=kCustom, calls=%fused_computation.272 | custom fusion | flops 786432 | bytes 66048 | tf_op jit(solution)/shard_map/transpose(jvp(jit(_take)))/scatter-add | solution.py:102
  913.9 16.1 %gather_fusion.19 = f32[6144,128]{1,0:T(8,128)S(1)} fusion(f32[128,128]{1,0:T(8,128)S(1)} %scatter_custom_fusion.21, s32[6144]{0:T(1024)S(1)} %copy-done.17), kind=kCustom, calls=%fused_computation.35 | custom fusion | bytes 6316032 | tf_op jit(solution)/shard_map/transpose(jvp())/gather | solution.py:101
  934.7 33.4 %scatter_custom_fusion.18 = f32[128,128]{1,0:T(8,128)S(1)} fusion(s32[6144]{0:T(1024)} %get-tuple-element.178, f32[6144,128]{1,0:T(8,128)S(1)} %copy.465, f32[]{:T(128)} %constant.138.clone.1), kind=kCustom, calls=%fused_computation.278 | custom fusion | flops 786432 | bytes 66048 | tf_op jit(solution)/shard_map/transpose(jvp(jit(_take)))/scatter-add | solution.py:102
  968.1 16.5 %gather_fusion.16 = f32[6144,128]{1,0:T(8,128)S(1)} fusion(f32[128,128]{1,0:T(8,128)S(1)} %scatter_custom_fusion.18, s32[6144]{0:T(1024)S(1)} %copy-done.17), kind=kCustom, calls=%fused_computation.32 | custom fusion | bytes 6316032 | tf_op jit(solution)/shard_map/transpose(jvp())/gather | solution.py:101
  989.3 33.4 %scatter_custom_fusion.22 = f32[128,128]{1,0:T(8,128)S(1)} fusion(s32[6144]{0:T(1024)} %get-tuple-element.178, f32[6144,128]{1,0:T(8,128)S(1)} %copy.473, f32[]{:T(128)} %constant.138.clone.1), kind=kCustom, calls=%fused_computation.270 | custom fusion | flops 786432 | bytes 66048 | tf_op jit(solution)/shard_map/transpose(jvp(jit(_take)))/scatter-add | solution.py:102
  1022.7 16.1 %gather_fusion.20 = f32[6144,128]{1,0:T(8,128)S(1)} fusion(f32[128,128]{1,0:T(8,128)S(1)} %scatter_custom_fusion.22, s32[6144]{0:T(1024)S(1)} %copy-done.17), kind=kCustom, calls=%fused_computation.36 | custom fusion | bytes 6316032 | tf_op jit(solution)/shard_map/transpose(jvp())/gather | solution.py:101
  1043.6 33.4 %scatter_custom_fusion.20 = f32[128,128]{1,0:T(8,128)S(1)} fusion(s32[6144]{0:T(1024)} %get-tuple-element.178, f32[6144,128]{1,0:T(8,128)S(1)} %copy.469, f32[]{:T(128)} %constant.138.clone.1), kind=kCustom, calls=%fused_computation.274 | custom fusion | flops 786432 | bytes 66048 | tf_op jit(solution)/shard_map/transpose(jvp(jit(_take)))/scatter-add | solution.py:102
  1077.0 16.1 %gather_fusion.18 = f32[6144,128]{1,0:T(8,128)S(1)} fusion(f32[128,128]{1,0:T(8,128)S(1)} %scatter_custom_fusion.20, s32[6144]{0:T(1024)S(1)} %copy-done.17), kind=kCustom, calls=%fused_computation.34 | custom fusion | bytes 6316032 | tf_op jit(solution)/shard_map/transpose(jvp())/gather | solution.py:101
  1097.9 33.4 %scatter_custom_fusion.19 = f32[128,128]{1,0:T(8,128)S(1)} fusion(s32[6144]{0:T(1024)} %get-tuple-element.178, f32[6144,128]{1,0:T(8,128)S(1)} %copy.467, f32[]{:T(128)} %constant.138.clone.1), kind=kCustom, calls=%fused_computation.276 | custom fusion | flops 786432 | bytes 66048 | tf_op jit(solution)/shard_map/transpose(jvp(jit(_take)))/scatter-add | solution.py:102
  1131.2 16.1 %gather_fusion.17 = f32[6144,128]{1,0:T(8,128)S(1)} fusion(f32[128,128]{1,0:T(8,128)S(1)} %scatter_custom_fusion.19, s32[6144]{0:T(1024)S(1)} %copy-done.17), kind=kCustom, calls=%fused_computation.33 | custom fusion | bytes 6316032 | tf_op jit(solution)/shard_map/transpose(jvp())/gather | solution.py:101
  1152.1 33.4 %scatter_custom_fusion.15 = f32[128,128]{1,0:T(8,128)S(1)} fusion(s32[6144]{0:T(1024)} %get-tuple-element.178, f32[6144,128]{1,0:T(8,128)S(1)} %copy.459, f32[]{:T(128)} %constant.138.clone.1), kind=kCustom, calls=%fused_computation.284 | custom fusion | flops 786432 | bytes 66048 | tf_op jit(solution)/shard_map/transpose(jvp(jit(_take)))/scatter-add | solution.py:102
  1185.5 16.3 %gather_fusion.13 = f32[6144,128]{1,0:T(8,128)S(1)} fusion(f32[128,128]{1,0:T(8,128)S(1)} %scatter_custom_fusion.15, s32[6144]{0:T(1024)S(1)} %copy-done.17), kind=kCustom, calls=%fused_computation.29 | custom fusion | bytes 6316032 | tf_op jit(solution)/shard_map/transpose(jvp())/gather | solution.py:101
  1204.1 33.5 %scatter_custom_fusion.23 = f32[128,128]{1,0:T(8,128)S(1)} fusion(s32[6144]{0:T(1024)} %get-tuple-element.178, f32[6144,128]{1,0:T(8,128)} %copy.476, f32[]{:T(128)} %constant.138.clone.1), kind=kCustom, calls=%fused_computation.268 | custom fusion | flops 786432 | bytes 66048 | tf_op jit(solution)/shard_map/transpose(jvp(jit(_take)))/scatter-add | solution.py:102
  1237.6 21.0 %gather_fusion.21 = f32[6144,128]{1,0:T(8,128)} fusion(f32[128,128]{1,0:T(8,128)S(1)} %scatter_custom_fusion.23, s32[6144]{0:T(1024)S(1)} %copy-done.17), kind=kCustom, calls=%fused_computation.37 | custom fusion | bytes 6316032 | tf_op jit(solution)/shard_map/transpose(jvp())/gather | solution.py:101
  1288.9 33.5 %scatter_custom_fusion.32 = f32[432,128]{1,0:T(8,128)S(1)} fusion(s32[6144]{0:T(1024)} %get-tuple-element.166, bf16[6144,128]{1,0:T(8,128)(2,1)S(1)} %convolution_convert_fusion.1, f32[]{:T(128)} %constant.138.clone.1), kind=kCustom, calls=%fused_computation.93 | custom fusion | flops 1572864 | bytes 1794560 | tf_op jit(solution)/shard_map/transpose(jvp(jit(_take)))/scatter-add | solution.py:89
  1333.8 33.5 %scatter_custom_fusion.25 = f32[3,432]{0,1:T(8,128)S(1)} fusion(s32[6144]{0:T(1024)} %get-tuple-element.166, f32[6144,3]{1,0:T(8,128)} %copy.481, f32[]{:T(128)} %constant.138.clone.1), kind=kCustom, calls=%fused_computation.223 | custom fusion | flops 18432 | bytes 5696 | tf_op jit(solution)/shard_map/transpose(jvp(jit(_take)))/scatter-add | solution.py:78
  1367.3 33.5 %scatter_custom_fusion.24 = f32[3,432]{0,1:T(8,128)S(1)} fusion(s32[6144]{0:T(1024)} %get-tuple-element.179, f32[6144,3]{1,0:T(8,128)} %copy.480, f32[]{:T(128)} %constant.138.clone.1), kind=kCustom, calls=%fused_computation.225 | custom fusion | flops 18432 | bytes 5696 | tf_op jit(solution)/shard_map/transpose(jvp(jit(_take)))/scatter-add | solution.py:78
  1403.9 33.4 %scatter_custom_fusion.31 = f32[128,128]{1,0:T(8,128)S(1)} fusion(s32[6144]{0:T(1024)} %get-tuple-element.178, bf16[6144,128]{1,0:T(8,128)(2,1)S(1)} %convolution_convert_fusion.1, f32[]{:T(128)} %constant.138.clone.1), kind=kCustom, calls=%fused_computation.95 | custom fusion | flops 1572864 | bytes 1638912 | tf_op jit(solution)/shard_map/transpose(jvp(jit(_take)))/scatter-add | solution.py:89
  1448.4 43.8 %scatter_custom_fusion.30 = f32[128]{0:T(128)} fusion(s32[6144]{0:T(1024)} %param.46, f32[6144]{0:T(1024)S(1)} %get-tuple-element.162, f32[]{:T(128)} %constant.138.clone.1), kind=kCustom, calls=%fused_computation.372 | custom fusion | flops 6144 | bytes 1024 | tf_op jit(solution)/shard_map/jvp()/scatter-add | solution.py:109
  (490 shorter events, 314.6 us)
Async XLA Ops:
  0.6 734.2 %copy-start = (bf16[256,128]{1,0:T(8,128)(2,1)S(1)}, bf16[256,128]{1,0:T(8,128)(2,1)}, u32[]{:S(2)}) copy-start(bf16[256,128]{1,0:T(8,128)(2,1)} %param.55) | copy-start | bytes 196612
  11.5 19.8 %collective-permute-start.1 = (f32[1,3,3,3,32]{4,3,2,1,0:T(4,128)S(1)}, f32[1,3,3,3,32]{4,3,2,1,0:T(4,128)S(1)}, u32[]{:S(2)}, u32[]{:S(2)}) collective-permute-start(f32[1,3,3,3,32]{4,3,2,1,0:T(4,128)S(1)} %bitcast.226), channel_id=1, source_target_pairs={{8,0},{16,8},{24,16},{0,24},{9,1},{17,9},{25,17},{1,25},{10,2},{18... | collective-permute-start | bytes 10376 | tf_op jit(solution)/shard_map/ppermute | solution.py:19
  14.0 17.4 %collective-permute-start = (f32[1,3,3,3,32]{4,3,2,1,0:T(4,128)S(1)}, f32[1,3,3,3,32]{4,3,2,1,0:T(4,128)S(1)}, u32[]{:S(2)}, u32[]{:S(2)}) collective-permute-start(f32[1,3,3,3,32]{4,3,2,1,0:T(4,128)S(1)} %bitcast.225), channel_id=1, source_target_pairs={{0,8},{8,16},{16,24},{24,0},{1,9},{9,17},{17,25},{25,1},{2,10},{10... | collective-permute-start | bytes 10376 | tf_op jit(solution)/shard_map/ppermute | solution.py:17
  20.6 20.8 %copy-start.96 = (bf16[128]{0:T(256)(128)(2,1)S(1)}, bf16[128]{0:T(256)(128)(2,1)}, u32[]{:S(2)}) copy-start(bf16[128]{0:T(256)(128)(2,1)} %param.56) | copy-start | bytes 772
  22.3 91.4 %collective-permute-start.7 = (f32[1,3,3,32,128]{4,3,2,1,0:T(8,128)}, f32[1,3,3,32,128]{4,3,2,1,0:T(8,128)}, u32[]{:S(2)}, u32[]{:S(2)}) collective-permute-start(f32[1,3,3,32,128]{4,3,2,1,0:T(8,128)} %bitcast.11), channel_id=1, source_target_pairs={{8,0},{16,8},{24,16},{0,24},{9,1},{17,9},{25,17},{1,25},{10,2},{18... | collective-permute-start | bytes 442376 | tf_op jit(solution)/shard_map/ppermute | solution.py:19
  24.0 89.7 %collective-permute-start.6 = (f32[1,3,3,32,128]{4,3,2,1,0:T(8,128)}, f32[1,3,3,32,128]{4,3,2,1,0:T(8,128)}, u32[]{:S(2)}, u32[]{:S(2)}) collective-permute-start(f32[1,3,3,32,128]{4,3,2,1,0:T(8,128)} %bitcast.9), channel_id=1, source_target_pairs={{0,8},{8,16},{16,24},{24,0},{1,9},{9,17},{17,25},{25,1},{2,10},{10... | collective-permute-start | bytes 442376 | tf_op jit(solution)/shard_map/ppermute | solution.py:17
  26.4 38.9 %copy-start.41 = (s32[6144]{0:T(1024)}, s32[6144]{0:T(1024)S(1)}, u32[]{:S(2)}) copy-start(s32[6144]{0:T(1024)S(1)} %get-tuple-element.167) | copy-start | bytes 73732
  31.4 6.0 collective-permute-start.2
  33.0 4.6 collective-permute-start.3
  38.2 19.9 %collective-permute-start.4 = (f32[5,5,1,3,32]{4,3,2,1,0:T(4,128)}, f32[5,5,1,3,32]{4,3,2,1,0:T(4,128)}, u32[]{:S(2)}, u32[]{:S(2)}) collective-permute-start(f32[5,5,1,3,32]{4,3,2,1,0:T(4,128)} %get-tuple-element.142), channel_id=1, source_target_pairs={{0,1},{1,0},{2,3},{3,2},{4,5},{5,4},{6,7},{7,6},{8,9},{9,8},{10,11... | collective-permute-start | bytes 28808 | tf_op jit(solution)/shard_map/ppermute | solution.py:17
  39.7 18.4 %collective-permute-start.5 = (f32[5,5,1,3,32]{4,3,2,1,0:T(4,128)}, f32[5,5,1,3,32]{4,3,2,1,0:T(4,128)}, u32[]{:S(2)}, u32[]{:S(2)}) collective-permute-start(f32[5,5,1,3,32]{4,3,2,1,0:T(4,128)} %get-tuple-element.143), channel_id=1, source_target_pairs={{1,0},{0,1},{3,2},{2,3},{5,4},{4,5},{7,6},{6,7},{9,8},{8,9},{11,10... | collective-permute-start | bytes 28808 | tf_op jit(solution)/shard_map/ppermute | solution.py:19
  42.0 21.8 %copy-start.90 = (f32[3,128]{1,0:T(4,128)S(1)}, f32[3,128]{1,0:T(4,128)}, u32[]{:S(2)}) copy-start(f32[3,128]{1,0:T(4,128)} %param.41) | copy-start | bytes 4612
  112.8 35.6 %copy-start.13 = (f32[27,32,128]{2,1,0:T(8,128)S(1)}, f32[27,32,128]{2,1,0:T(8,128)}, u32[]{:S(2)}) copy-start(f32[27,32,128]{2,1,0:T(8,128)} %pad_maximum_fusion.2) | copy-start | bytes 1327108
  113.0 37.9 %copy-start.42 = (f32[6144]{0:T(1024)}, f32[6144]{0:T(1024)S(1)}, u32[]{:S(2)}) copy-start(f32[6144]{0:T(1024)S(1)} %get-tuple-element.100) | copy-start | bytes 73732
  114.8 10.8 collective-permute-start.8
  115.8 12.3 collective-permute-start.9
  118.8 22.8 %copy-start.32 = (f32[3,6144]{1,0:T(4,128)}, f32[3,6144]{1,0:T(4,128)S(1)}, u32[]{:S(2)}) copy-start(f32[3,6144]{1,0:T(4,128)S(1)} %broadcast_divide_fusion) | copy-start | bytes 221188
  129.1 12.5 collective-permute-start.10
  130.7 17.7 %collective-permute-start.11 = (f32[5,5,1,32,128]{4,3,2,1,0:T(8,128)S(1)}, f32[5,5,1,32,128]{4,3,2,1,0:T(8,128)S(1)}, u32[]{:S(2)}, u32[]{:S(2)}) collective-permute-start(f32[5,5,1,32,128]{4,3,2,1,0:T(8,128)S(1)} %get-tuple-element.127), channel_id=1, source_target_pairs={{1,0},{0,1},{3,2},{2,3},{5,4},{4,5},{7,6},{6,7},{9,8},{8,9},{11,10... | collective-permute-start | bytes 1228808 | tf_op jit(solution)/shard_map/ppermute | solution.py:19
  163.1 23.2 %copy-start.37 = (f32[6144]{0:T(1024)S(1)}, f32[6144]{0:T(1024)}, u32[]{:S(2)}) copy-start(f32[6144]{0:T(1024)} %copy-done.36) | copy-start | bytes 73732
  163.1 23.2 %copy-start.69 = (f32[6144]{0:T(1024)S(1)}, f32[6144]{0:T(1024)}, u32[]{:S(2)}) copy-start(f32[6144]{0:T(1024)} %get-tuple-element.170) | copy-start | bytes 73732
  163.1 23.2 %copy-start.74 = (pred[6144]{0:T(1024)(128)(4,1)S(1)}, pred[6144]{0:T(1024)(128)(4,1)}, u32[]{:S(2)}) copy-start(pred[6144]{0:T(1024)(128)(4,1)} %get-tuple-element.187) | copy-start | bytes 18436
  163.1 23.2 %copy-start.91 = (f32[8,128]{1,0:T(8,128)S(1)}, f32[8,128]{1,0:T(8,128)}, u32[]{:S(2)}) copy-start(f32[8,128]{1,0:T(8,128)} %param.51) | copy-start | bytes 12292
  163.1 23.2 %copy-start.92 = (f32[8]{0:T(128)S(1)}, f32[8]{0:T(128)}, u32[]{:S(2)}) copy-start(f32[8]{0:T(128)} %convert_multiply_fusion.4) | copy-start | bytes 100
  203.5 123.3 %copy-start.2 = (f32[6144,128]{0,1:T(8,128)}, f32[6144,128]{0,1:T(8,128)S(1)}, u32[]{:S(2)}) copy-start(f32[6144,128]{0,1:T(8,128)S(1)} %get-tuple-element.99) | copy-start | bytes 9437188
  771.7 36.0 %copy-start.17 = (s32[6144]{0:T(1024)S(1)}, s32[6144]{0:T(1024)}, u32[]{:S(2)}) copy-start(s32[6144]{0:T(1024)} %get-tuple-element.175) | copy-start | bytes 73732
  1283.9 38.4 %copy-start.22 = (f32[128,128]{1,0:T(8,128)S(1)}, f32[128,128]{1,0:T(8,128)}, u32[]{:S(2)}) copy-start(f32[128,128]{1,0:T(8,128)} %param.50) | copy-start | bytes 196612
  1283.9 38.8 %copy-start.80 = (s32[6]{0:T(128)S(1)}, s32[6]{0:T(128)}, u32[]{:S(2)}) copy-start(s32[6]{0:T(128)} %constant.297) | copy-start | bytes 76
  1288.8 34.9 %copy-start.83 = (s32[8]{0:T(128)S(1)}, s32[8]{0:T(128)}, u32[]{:S(2)}) copy-start(s32[8]{0:T(128)} %constant.299) | copy-start | bytes 100
  1288.8 35.7 %copy-start.86 = (s32[12]{0:T(128)S(1)}, s32[12]{0:T(128)}, u32[]{:S(2)}) copy-start(s32[12]{0:T(128)} %constant.298) | copy-start | bytes 148
  1331.6 69.8 %copy-start.84 = (s32[8]{0:T(128)S(1)}, s32[8]{0:T(128)}, u32[]{:S(2)}) copy-start(s32[8]{0:T(128)} %constant.299) | copy-start | bytes 100
  1331.6 70.6 %copy-start.87 = (s32[12]{0:T(128)S(1)}, s32[12]{0:T(128)}, u32[]{:S(2)}) copy-start(s32[12]{0:T(128)} %constant.298) | copy-start | bytes 148
  1331.6 71.5 %copy-start.81 = (s32[6]{0:T(128)S(1)}, s32[6]{0:T(128)}, u32[]{:S(2)}) copy-start(s32[6]{0:T(128)} %constant.297) | copy-start | bytes 76
  1331.6 105.8 %copy-start.40 = (f32[128,128]{1,0:T(8,128)S(1)}, f32[128,128]{1,0:T(8,128)}, u32[]{:S(2)}) copy-start(f32[128,128]{1,0:T(8,128)} %param.49) | copy-start | bytes 196612
  1333.8 105.8 %copy-start.89 = (f32[27]{0:T(128)S(1)}, f32[27]{0:T(128)}, u32[]{:S(2)}) copy-start(f32[27]{0:T(128)} %copy-done.88) | copy-start | bytes 328
  1437.7 56.7 %collective-permute-start.19 = (f32[1,3,3,32,128]{4,3,2,1,0:T(8,128)S(1)}, f32[1,3,3,32,128]{4,3,2,1,0:T(8,128)S(1)}, u32[]{:S(2)}, u32[]{:S(2)}) collective-permute-start(f32[1,3,3,32,128]{4,3,2,1,0:T(8,128)S(1)} %bitcast.201), channel_id=1, source_target_pairs={{8,0},{16,8},{24,16},{0,24},{9,1},{17,9},{25,17},{1,25},{10,2},{18... | collective-permute-start | bytes 442376 | tf_op jit(solution)/shard_map/ppermute | solution.py:19
  1437.8 56.6 %collective-permute-start.18 = (f32[1,3,3,32,128]{4,3,2,1,0:T(8,128)S(1)}, f32[1,3,3,32,128]{4,3,2,1,0:T(8,128)S(1)}, u32[]{:S(2)}, u32[]{:S(2)}) collective-permute-start(f32[1,3,3,32,128]{4,3,2,1,0:T(8,128)S(1)} %bitcast.200), channel_id=1, source_target_pairs={{0,8},{8,16},{16,24},{24,0},{1,9},{9,17},{17,25},{25,1},{2,10},{10... | collective-permute-start | bytes 442376 | tf_op jit(solution)/shard_map/ppermute | solution.py:17
  1438.3 3.3 collective-permute-start.13
  1439.6 4.6 collective-permute-start.12
  1444.3 48.0 %collective-permute-start.14 = (f32[5,1,3,3,32]{4,3,2,1,0:T(4,128)S(1)}, f32[5,1,3,3,32]{4,3,2,1,0:T(4,128)S(1)}, u32[]{:S(2)}, u32[]{:S(2)}) collective-permute-start(f32[5,1,3,3,32]{4,3,2,1,0:T(4,128)S(1)} %get-tuple-element.150), channel_id=1, source_target_pairs={{0,2},{2,4},{4,6},{6,0},{1,3},{3,5},{5,7},{7,1},{8,10},{10,12},{12... | collective-permute-start | bytes 17288 | tf_op jit(solution)/shard_map/ppermute | solution.py:17
  1446.4 45.9 %collective-permute-start.15 = (f32[5,1,3,3,32]{4,3,2,1,0:T(4,128)S(1)}, f32[5,1,3,3,32]{4,3,2,1,0:T(4,128)S(1)}, u32[]{:S(2)}, u32[]{:S(2)}) collective-permute-start(f32[5,1,3,3,32]{4,3,2,1,0:T(4,128)S(1)} %get-tuple-element.151), channel_id=1, source_target_pairs={{2,0},{4,2},{6,4},{0,6},{3,1},{5,3},{7,5},{1,7},{10,8},{12,10},{14... | collective-permute-start | bytes 17288 | tf_op jit(solution)/shard_map/ppermute | solution.py:19
  1492.3 6.0 collective-permute-start.16
  1493.9 4.4 collective-permute-start.17
  1494.4 10.7 collective-permute-start.20
  1494.8 11.8 collective-permute-start.21
  1506.6 12.5 collective-permute-start.22
  1508.3 16.2 %collective-permute-start.23 = (f32[5,5,1,32,128]{4,3,2,1,0:T(8,128)S(1)}, f32[5,5,1,32,128]{4,3,2,1,0:T(8,128)}, u32[]{:S(2)}, u32[]{:S(2)}) collective-permute-start(f32[5,5,1,32,128]{4,3,2,1,0:T(8,128)S(1)} %get-tuple-element.125), channel_id=1, source_target_pairs={{1,0},{0,1},{3,2},{2,3},{5,4},{4,5},{7,6},{6,7},{9,8},{8,9},{11,10... | collective-permute-start | bytes 1228808 | tf_op jit(solution)/shard_map/ppermute | solution.py:19
  1511.6 20.1 %copy-start.1 = (bf16[256,128]{1,0:T(8,128)(2,1)S(1)}, bf16[256,128]{1,0:T(8,128)(2,1)}, u32[]{:S(2)}) copy-start(bf16[256,128]{1,0:T(8,128)(2,1)} %param.55) | copy-start | bytes 196612
  (75 other events, 449.1 us)
where the time goes:
time: 1540 us; the launch traced here: 1530 us
  other arithmetic  856 us (56%)
  local copies, waits for them, and re-layouts  545 us (35%)
  waiting for transfers between devices  48.6 us (3%)
  matrix products  48.4 us (3%)
  starting transfers between devices  30.1 us (2%)
    scatter-add x9, other arithmetic, local_energy(): jax.ops.segment_sum(env_weight * comp[:, None], centre, num_segments=n_own)  301 us
    scatter-add x9, other arithmetic, local_energy(): total = total + comp[:, None] * jnp.take(env_m, centre, axis=0)  301 us
    gather x18, local copies, waits for them, and re-layouts, local_energy(): total = total + comp[:, None] * jnp.take(env_m, centre, axis=0)  184 us
    gather x18, local copies, waits for them, and re-layouts, local_energy(): jax.ops.segment_sum(env_weight * comp[:, None], centre, num_segments=n_own)  173 us
    scatter-add x2, other arithmetic, local_energy(): disp = jnp.take(pos_tab, other, axis=1) - jnp.take(pos_tab, centre, axis=1)  67 us
    gather x4, local copies, waits for them, and re-layouts, local_energy(): disp = jnp.take(pos_tab, other, axis=1) - jnp.take(pos_tab, centre, axis=1)  47.5 us
    scatter-add x1, other arithmetic, local_energy(): atom_energy = jax.ops.segment_sum(edge_energy, centre, num_segments=n_own)  43.8 us
    scatter-add x1, other arithmetic, local_energy(): jnp.take(proj_b, other, axis=0)  33.5 us
  transfers between devices with their start and end apart: 24, of which 12 were waited for; matrix products, arithmetic and copies ran while one was open for 9% of the time, Pallas kernels for 0%

commit v1 on v0

v1 whole, which is shorter than its diff:
```python
import math

import jax
import jax.numpy as jnp
from jax import lax
from jax.experimental import pallas as pl
from jax.experimental.pallas import tpu as pltpu
from jax.sharding import PartitionSpec as P

F32 = jnp.float32
BF16 = jnp.bfloat16
HIGH = lax.Precision.HIGHEST
AXES = ("gx", "gy", "gz")
CHUNK = 1024
SUB = 256
WIN = 16
OTHER_BITS = 9
OTHER_MASK = (1 << OTHER_BITS) - 1
LANES = 128
ROOT3 = 1.732


def dot_nn(a, b, precision=None):
    return lax.dot_general(
        a, b, (((1,), (0,)), ((), ())), preferred_element_type=F32, precision=precision
    )


def dot_nt(a, b, precision=None):
    return lax.dot_general(
        a, b, (((1,), (1,)), ((), ())), preferred_element_type=F32, precision=precision
    )


def dot_tn(a, b, precision=None):
    return lax.dot_general(
        a, b, (((0,), (0,)), ((), ())), preferred_element_type=F32, precision=precision
    )


def offset_classes():
    classes = [[], [], []]
    for a in (-1, 0, 1):
        for b in (-1, 0, 1):
            for c in (-1, 0, 1):
                if (a, b, c) != (0, 0, 0):
                    classes[abs(a) + abs(b) + abs(c) - 1].append((a, b, c))
    return classes


CLASSES = offset_classes()


def kind(off):
    return abs(off[0]) + abs(off[1]) + abs(off[2]) - 1


def z_blocks(s):
    blocks = []
    for t in (1, -1):
        blocks += [(0, t, s), (-1, t, s), (1, t, s)]
    return blocks + [(0, 0, s), (-1, 0, s), (1, 0, s)]


def y_own(s):
    return [(0, s, 0), (-1, s, 0), (1, s, 0)]


def y_blocks(s):
    blocks = y_own(s)
    for t in (1, -1):
        blocks += [(0, s, t), (-1, s, t), (1, s, t)]
    return blocks


def x_own(s):
    return [(s, 0, 0)]


def x_blocks(s):
    blocks = x_own(s)
    for t in (1, -1):
        blocks += [(s, t, 0), (s, t, 1), (s, t, -1)]
    return blocks + [(s, 0, 1), (s, 0, -1)]


SEND_GROUPS = [z_blocks(1), z_blocks(-1), y_own(1), y_own(-1), x_own(1), x_own(-1)]


class Plan:
    def __init__(self, widths):
        self.widths = widths

    def live(self, off):
        return self.widths[kind(off)]

    def rows(self, off):
        return -(-self.live(off) // 8) * 8

    def total(self, blocks):
        return sum(self.rows(off) for off in blocks)

    def start(self, blocks, off):
        at = 0
        for other in blocks:
            if other == off:
                return at
            at += self.rows(other)
        raise KeyError(off)

    def find(self, off):
        if off[0] != 0:
            return "x", off[0], self.start(x_blocks(off[0]), off)
        if off[1] != 0:
            return "y", off[1], self.start(y_blocks(off[1]), off)
        return "z", off[2], self.start(z_blocks(off[2]), off)

    def piece(self, messages, off, axis):
        if axis == "x" and off[1] != 0:
            axis, sign, at = "y", off[1], self.start(y_blocks(off[1]), off)
        else:
            axis, sign, at = "z", off[2], self.start(z_blocks(off[2]), off)
        return lax.slice_in_dim(messages[axis, sign], at, at + self.rows(off), axis=0)


def swap(plus, minus, axis, size, back=False):
    up = [(i, (i + 1) % size) for i in range(size)]
    down = [((i + 1) % size, i) for i in range(size)]
    if back:
        up, down = down, up
    if size <= 2:
        both = lax.ppermute(jnp.concatenate([plus, minus], axis=0), axis, up)
        rows = plus.shape[0]
        return both[:rows], both[rows:]
    return lax.ppermute(plus, axis, up), lax.ppermute(minus, axis, down)


def prep_kernel(plan, pos_ref, feat_ref, wa_ref, wb_ref, face_ref, edge_ref, corner_ref, *outs):
    pa_ref, pb_ref, sel_ref = outs[:3]
    sends = outs[3:9]
    own = feat_ref.shape[0]
    feat = feat_ref[...]
    pa_ref[...] = dot_nn(feat, wa_ref[...], HIGH)
    pb_ref[:, 0:LANES] = dot_nn(feat, wb_ref[...], HIGH)
    pos = jnp.concatenate([pos_ref[...], jnp.zeros((LANES - 3, own), F32)], axis=0)
    pb_ref[:, LANES:] = pos.T
    lists = (face_ref, edge_ref, corner_ref)
    lane = lax.broadcasted_iota(jnp.int32, (1, own), 1)
    sel_ref[...] = jnp.zeros_like(sel_ref)
    at = 0
    for blocks in SEND_GROUPS:
        for off in blocks:
            ref = lists[kind(off)]
            key = CLASSES[kind(off)].index(off)
            for j in range(plan.live(off)):
                row = ref[0, key, j]
                sel_ref[at + j : at + j + 1, :] = (lane == row).astype(F32)
            at += plan.rows(off)
    packed = dot_nn(sel_ref[...], pb_ref[...], HIGH)
    at = 0
    for blocks, send in zip(SEND_GROUPS, sends):
        rows = plan.total(blocks)
        send[...] = packed[at : at + rows, :]
        at += rows


def harmonics(ux, uy, uz):
    return [
        ux,
        uy,
        uz,
        ROOT3 * ux * uy,
        ROOT3 * uy * uz,
        ROOT3 * ux * uz,
        0.866 * (ux * ux - uy * uy),
        0.5 * (3.0 * uz * uz - 1.0),
    ]


def trig(half):
    turns = jnp.round(half)
    x = math.pi * (half - turns)
    odd = turns - 2.0 * jnp.floor(0.5 * turns)
    sign = 1.0 - 2.0 * odd
    x2 = x * x
    s = jnp.full_like(x, -1.0 / 39916800)
    for coef in (1.0 / 362880, -1.0 / 5040, 1.0 / 120, -1.0 / 6, 1.0):
        s = s * x2 + coef
    c = jnp.full_like(x, 1.0 / 479001600)
    for coef in (-1.0 / 3628800, 1.0 / 40320, -1.0 / 720, 1.0 / 24, -0.5, 1.0):
        c = c * x2 + coef
    return sign * x * s, sign * c


def waves(half, count):
    s1, c1 = trig(half)
    sins, coss = [s1], [c1]
    s0, c0 = jnp.zeros_like(s1), jnp.ones_like(c1)
    for _ in range(count - 1):
        sn = 2.0 * c1 * sins[-1] - s0
        cn = 2.0 * c1 * coss[-1] - c0
        s0, c0 = sins[-1], coss[-1]
        sins.append(sn)
        coss.append(cn)
    return sins, coss


def look_up(table_row, index):
    low = index & (LANES - 1)
    high = index >> 7
    result = jnp.zeros(index.shape, F32)
    for block in range(table_row.shape[1] // LANES):
        part = jnp.broadcast_to(table_row[:, block * LANES : (block + 1) * LANES], index.shape)
        got = jnp.take_along_axis(part, low, axis=1)
        result = jnp.where(high == block, got, result)
    return result


def in_lanes(tile):
    return jnp.concatenate([tile[r : r + 1, :] for r in range(tile.shape[0])], axis=1)


def one_hot(row, base, count):
    near = jnp.clip(row - base, -1, LANES).astype(BF16)
    iota = lax.broadcasted_iota(jnp.int32, (count, row.shape[1]), 0).astype(BF16)
    return jnp.where(iota == near, jnp.ones((), BF16), jnp.zeros((), BF16))


def split(x):
    high = x.astype(BF16).astype(F32)
    return high, x - high


def main_kernel(plan, *refs):
    (
        count_ref,
        skey_ref,
        key_ref,
        pa_ref,
        pb_ref,
        zp_ref,
        zm_ref,
        yp_ref,
        ym_ref,
        xp_ref,
        xm_ref,
        wa_ref,
        wb_ref,
        wrad_ref,
        w1_ref,
        wenv_ref,
        wval_ref,
        w2_ref,
        wout_ref,
        energy_ref,
        fg_ref,
        force_ref,
        rxp_ref,
        rxm_ref,
        ryp_ref,
        rym_ref,
        rzp_ref,
        rzm_ref,
        tab_ref,
        table_ref,
        w1t_ref,
        wevt_ref,
        w2t_ref,
        wev_ref,
        wradb_ref,
        wcol_ref,
        y_ref,
        basis_ref,
        geo_ref,
        first_ref,
        dsilu_ref,
        ew_ref,
        val_ref,
        a_ref,
        env_ref,
        denv_ref,
        big_ref,
        dt_ref,
        dv_ref,
        dfa_ref,
        dmix_env_ref,
        ae_ref,
        dy_ref,
        db_ref,
        dr_ref,
        acc_ref,
    ) = refs
    own, chans = pa_ref.shape
    n_basis = wrad_ref.shape[0]
    rows_all = key_ref.shape[0]
    per = CHUNK // LANES
    subs = CHUNK // SUB
    sub_rows = SUB // LANES
    messages = {
        ("z", 1): zp_ref,
        ("z", -1): zm_ref,
        ("y", 1): yp_ref,
        ("y", -1): ym_ref,
        ("x", 1): xp_ref,
        ("x", -1): xm_ref,
    }
    n_ghost = sum(len(c) * w for c, w in zip(CLASSES, plan.widths))
    n_tab = own + n_ghost
    n_sel = own + n_tab

    tab_ref[...] = jnp.zeros_like(tab_ref)
    tab_ref[0:own, 0:chans] = pa_ref[...]
    tab_ref[own : 2 * own, :] = pb_ref[...]
    at = 2 * own
    for group in CLASSES:
        for off in group:
            axis, sign, begin = plan.find(off)
            live = plan.live(off)
            tab_ref[at : at + live, :] = messages[axis, sign][begin : begin + live, :]
            at += live
    pos_t = tab_ref[own : own + 4 * LANES, LANES:].T
    rad = wrad_ref[...]
    rad_hi, rad_lo = split(rad)
    pad_at = n_sel
    tab_ref[pad_at : pad_at + n_basis, 0:chans] = rad_hi
    tab_ref[pad_at + n_basis : pad_at + 2 * n_basis, 0:chans] = rad_hi
    tab_ref[pad_at + 2 * n_basis : pad_at + 3 * n_basis, 0:chans] = rad_lo
    table_ref[...] = tab_ref[0 : table_ref.shape[1], 0:chans].T.astype(BF16)

    def flip(w):
        return w.astype(F32).T.astype(BF16)

    w1t_ref[...] = flip(w1_ref[...])
    wevt_ref[0:chans, :] = flip(wenv_ref[...])
    wevt_ref[chans:, :] = flip(wval_ref[...])
    w2t_ref[:, 0:chans] = flip(w2_ref[0:chans, :])
    w2t_ref[:, chans:] = flip(w2_ref[chans:, :])
    wev_ref[:, 0:chans] = wenv_ref[...]
    wev_ref[:, chans:] = wval_ref[...]
    wradb_ref[...] = jnp.concatenate([rad, jnp.zeros_like(rad)], axis=0).astype(BF16)
    wcol_ref[...] = jnp.broadcast_to(wout_ref[...].astype(F32), (chans, LANES)).T

    keys = key_ref[...]
    centre = keys >> OTHER_BITS
    other = keys & OTHER_MASK
    valid = (keys != (own - 1) * (OTHER_MASK + 1) + OTHER_MASK).astype(F32)
    r = [
        look_up(pos_t[a : a + 1, :], other) - look_up(pos_t[a : a + 1, 0:LANES], centre)
        for a in range(3)
    ]
    d2 = r[0] * r[0] + r[1] * r[1] + r[2] * r[2] + 0.01
    dist = jnp.sqrt(d2)
    inv = 1.0 / dist
    q = 1.0 / (1.0 + 0.25 * d2)
    envelope = q * q
    unit = [x * inv for x in r]
    for m, comp in enumerate(harmonics(*unit)):
        y_ref[pl.ds(m, rows_all, stride=8), :] = comp
    sins, _ = waves(0.5 * dist, n_basis)
    scale = envelope * inv
    for n in range(n_basis):
        basis_ref[pl.ds(n, rows_all, stride=n_basis), :] = sins[n] * scale
    for i, plane in enumerate((unit[0], unit[1], unit[2], dist, inv, q, envelope * valid, valid)):
        geo_ref[i] = plane

    env_ref[...] = jnp.zeros_like(env_ref)
    denv_ref[...] = jnp.zeros_like(denv_ref)
    ae_ref[...] = jnp.zeros_like(ae_ref)
    acc_ref[...] = jnp.zeros_like(acc_ref)
    dr_ref[...] = jnp.zeros_like(dr_ref)

    n_chunks = lax.div(count_ref[0] + (CHUNK - 1), jnp.int32(CHUNK))

    def window(k, s):
        row = k * per + s * sub_rows
        low = skey_ref[row, 0] >> OTHER_BITS
        high = skey_ref[row + sub_rows - 1, LANES - 1] >> OTHER_BITS
        start = pl.multiple_of((low >> 3) << 3, 8)
        more = lax.div(high - start, jnp.int32(WIN))
        return start, more

    def any_more(k):
        most = window(k, 0)[1]
        for s in range(1, subs):
            most = jnp.maximum(most, window(k, s)[1])
        return most > 0

    def select(k, s, start):
        row = k * per + s * sub_rows
        crow = in_lanes(key_ref[pl.ds(row, sub_rows), :] >> OTHER_BITS) - start
        hot = lax.broadcasted_iota(jnp.int32, (WIN, SUB), 0) == crow
        tiles = [
            y_ref[pl.ds(pl.multiple_of((row + j) * 8, 8), 8), :] for j in range(sub_rows)
        ]
        ys = jnp.concatenate(tiles, axis=1)
        parts = [hot.astype(F32)]
        for m in range(8):
            parts.append(jnp.where(hot, ys[m : m + 1, :], 0.0))
        return jnp.concatenate(parts, axis=0).astype(BF16)

    def load_window(ref, start):
        return jnp.concatenate(
            [ref[m, pl.ds(start, WIN), :] for m in range(9)], axis=0
        ).astype(BF16)

    def add_window(ref, start, rows):
        for m in range(9):
            ref[m, pl.ds(start, WIN), :] += rows[m * WIN : (m + 1) * WIN, :]

    def sub_lanes(s):
        return slice(s * SUB, (s + 1) * SUB)

    def more_windows(k, body):
        @pl.when(any_more(k))
        def _():
            for s in range(subs):
                start, more = window(k, s)

                def step(t, carry, s=s, start=start):
                    body(s, pl.multiple_of(start + t * WIN, 8))
                    return carry

                lax.fori_loop(1, more + 1, step, 0)

    def row_of(plane, k):
        return in_lanes(geo_ref[plane, pl.ds(pl.multiple_of(k * per, 8), per), :])

    def phase_a(k, carry):
        kt = key_ref[pl.ds(pl.multiple_of(k * per, 8), per), :]
        crow = in_lanes(kt >> OTHER_BITS)
        orow = in_lanes(kt & OTHER_MASK)
        hots = [one_hot(crow, 0, own)]
        for base in range(0, n_tab, LANES):
            hots.append(one_hot(orow, base, min(LANES, n_tab - base)))
        tiles = [
            basis_ref[pl.ds(pl.multiple_of((k * per + j) * n_basis, 8), n_basis), :]
            for j in range(per)
        ]
        basis = jnp.concatenate(tiles, axis=1)
        b_hi, b_lo = split(basis)
        hots.append(jnp.concatenate([b_hi, b_lo], axis=0).astype(BF16))
        hots.append(jnp.concatenate([b_hi, jnp.zeros_like(b_hi)], axis=0).astype(BF16))
        mixed = dot_nn(table_ref[...], jnp.concatenate(hots, axis=0)).astype(BF16)
        z1 = dot_nn(w1t_ref[...], mixed)
        sg = 0.5 + 0.5 * jnp.tanh(0.5 * z1)
        first = z1 * sg
        dsilu_ref[k] = (sg + first * (1.0 - sg)).astype(BF16)
        first = first.astype(BF16)
        first_ref[k] = first
        both = dot_nn(wevt_ref[...], first)
        ew = (both[0:chans] * row_of(6, k)).astype(BF16)
        ew_ref[k] = ew
        val_ref[k] = both[chans:].astype(BF16)
        for s in range(subs):
            start, _ = window(k, s)
            a = select(k, s, start)
            a_ref[k * subs + s] = a
            add_window(env_ref, start, dot_nt(a, ew[:, sub_lanes(s)]))

        def again(s, start):
            a = select(k, s, start)
            add_window(env_ref, start, dot_nt(a, ew_ref[k, :, sub_lanes(s)]))

        more_windows(k, again)
        return carry

    lax.fori_loop(0, n_chunks, phase_a, 0)

    def phase_b(k, carry):
        for s in range(subs):
            start, _ = window(k, s)
            big_ref[:, sub_lanes(s)] = dot_tn(load_window(env_ref, start), a_ref[k * subs + s])

        def again_total(s, start):
            big_ref[:, sub_lanes(s)] += dot_tn(load_window(env_ref, start), select(k, s, start))

        more_windows(k, again_total)
        total = 0.2 * big_ref[...]
        value = val_ref[k].astype(F32)
        scalar = (value * total).astype(BF16)
        z2 = dot_nn(w2t_ref[...], jnp.concatenate([first_ref[k], scalar], axis=0))
        sg = 0.5 + 0.5 * jnp.tanh(0.5 * z2)
        second = z2 * sg
        wcol = jnp.concatenate([wcol_ref[...]] * per, axis=1)
        ee = jnp.sum(second.astype(BF16).astype(F32) * wcol, axis=0, keepdims=True)
        envv = row_of(6, k)
        dy_ref[9, :, :] = jnp.zeros((per, LANES), F32)
        live = ee * row_of(7, k)
        for j in range(per):
            dmix_env_ref[k, j : j + 1, :] = live[:, j * LANES : (j + 1) * LANES]
        energy = ee * envv
        dz2 = ((wcol * envv) * (sg + second * (1.0 - sg))).astype(BF16)
        dj = dot_nn(w2_ref[...], dz2)
        dfa_ref[k] = dj[0:chans].astype(BF16)
        dscalar = dj[chans:]
        dt = (0.2 * value * dscalar).astype(BF16)
        dt_ref[k] = dt
        dv_ref[k] = (total * dscalar).astype(BF16)

        def add_energy(s, start):
            row = k * per + s * sub_rows
            crow = in_lanes(key_ref[pl.ds(row, sub_rows), :] >> OTHER_BITS) - start
            hot = lax.broadcasted_iota(jnp.int32, (WIN, SUB), 0) == crow
            part = jnp.where(hot, energy[:, sub_lanes(s)], 0.0)
            half = part[:, 0:LANES]
            for j in range(1, sub_rows):
                half = half + part[:, j * LANES : (j + 1) * LANES]
            ae_ref[pl.ds(start, WIN), :] += half

        for s in range(subs):
            start, _ = window(k, s)
            add_window(denv_ref, start, dot_nt(a_ref[k * subs + s], dt[:, sub_lanes(s)]))
            add_energy(s, start)

        def again(s, start):
            add_window(
                denv_ref, start, dot_nt(select(k, s, start), dt_ref[k, :, sub_lanes(s)])
            )
            add_energy(s, start)

        more_windows(k, again)
        return carry

    lax.fori_loop(0, n_chunks, phase_b, 0)

    def phase_c(k, carry):
        def env_terms(s, start, a, fresh):
            e_win = load_window(env_ref, start)
            d_win = load_window(denv_ref, start)
            dew = dot_tn(d_win, a)
            pair = jnp.concatenate(
                [dt_ref[k, :, sub_lanes(s)], ew_ref[k, :, sub_lanes(s)]], axis=0
            )
            prods = dot_nn(jnp.concatenate([e_win, d_win], axis=1), pair)
            hot = a[0:WIN].astype(F32)
            if fresh:
                big_ref[:, sub_lanes(s)] = dew
            else:
                big_ref[:, sub_lanes(s)] += dew
            for m in range(1, 9):
                row = jnp.sum(prods[m * WIN : (m + 1) * WIN] * hot, axis=0, keepdims=True)
                for j in range(sub_rows):
                    at = s * sub_rows + j
                    piece = row[:, j * LANES : (j + 1) * LANES]
                    if fresh:
                        dy_ref[m, at : at + 1, :] = piece
                    else:
                        dy_ref[m, at : at + 1, :] += piece

        for s in range(subs):
            start, _ = window(k, s)
            env_terms(s, start, a_ref[k * subs + s], True)
        more_windows(k, lambda s, start: env_terms(s, start, select(k, s, start), False))
        dew = big_ref[...]
        dpre = (dew * row_of(6, k)).astype(BF16)
        denv_row = jnp.sum(dew * ew_ref[k].astype(F32), axis=0, keepdims=True)
        for j in range(per):
            dy_ref[0, j : j + 1, :] = denv_row[:, j * LANES : (j + 1) * LANES]
        dfirst = dfa_ref[k].astype(F32) + dot_nn(
            wev_ref[...], jnp.concatenate([dpre, dv_ref[k]], axis=0)
        )
        dz1 = (dfirst * dsilu_ref[k].astype(F32)).astype(BF16)
        dmixed = dot_nn(w1_ref[...], dz1).astype(BF16)
        dbasis = dot_nn(wradb_ref[...], dmixed)
        for j in range(per):
            db_ref[j * n_basis : (j + 1) * n_basis, :] = dbasis[
                0:n_basis, j * LANES : (j + 1) * LANES
            ]
        tile = pl.ds(pl.multiple_of(k * per, 8), per)
        ux, uy, uz, dist, inv, q = [geo_ref[i, tile, :] for i in range(6)]
        envelope = q * q
        g = envelope * inv
        denvelope = -(q * envelope) * dist
        dg = (denvelope - g) * inv
        sins, coss = waves(0.5 * dist, n_basis)
        denv_direct = dmix_env_ref[k] + dy_ref[0] / envelope
        ddist = denv_direct * denvelope
        for n in range(n_basis):
            db = db_ref[pl.ds(n, per, stride=n_basis), :]
            ddist = ddist + db * (coss[n] * ((n + 1) * math.pi / 2.0) * g + sins[n] * dg)
        y = [dy_ref[m] for m in range(9)]
        gx = y[1] + ROOT3 * (uy * y[4] + uz * y[6]) + (2.0 * 0.866) * ux * y[7]
        gy = y[2] + ROOT3 * (ux * y[4] + uz * y[5]) - (2.0 * 0.866) * uy * y[7]
        gz = y[3] + ROOT3 * (uy * y[5] + ux * y[6]) + 3.0 * uz * y[8]
        along = ddist - inv * (gx * ux + gy * uy + gz * uz)
        for i, (gu, u) in enumerate(((gx, ux), (gy, uy), (gz, uz))):
            hi, lo = split(inv * gu + along * u)
            dr_ref[pl.ds(i, per, stride=16), :] = hi
            dr_ref[pl.ds(3 + i, per, stride=16), :] = lo
        dr = jnp.concatenate([dr_ref[j * 16 : (j + 1) * 16, :] for j in range(per)], axis=1)
        kt = key_ref[tile, :]
        crow = in_lanes(kt >> OTHER_BITS)
        orow = in_lanes(kt & OTHER_MASK)
        hots = [one_hot(crow, 0, own)]
        for base in range(0, n_tab, LANES):
            hots.append(one_hot(orow, base, min(LANES, n_tab - base)))
        sums = dot_nt(
            jnp.concatenate(hots, axis=0),
            jnp.concatenate([dmixed, dr.astype(BF16)], axis=0),
        )
        acc_ref[:, 0:chans] += sums[:, 0:chans]
        acc_ref[:, chans : chans + 16] += sums[:, chans:]
        return carry

    lax.fori_loop(0, n_chunks, phase_c, 0)

    energy_ref[...] = jnp.sum(ae_ref[0:own, :].T, axis=0, keepdims=True)
    fg_ref[...] = dot_nt(acc_ref[0:own, 0:chans], wa_ref[...], HIGH) + dot_nt(
        acc_ref[own : 2 * own, 0:chans], wb_ref[...], HIGH
    )
    force_ref[...] = acc_ref[own : 2 * own, LANES:] - acc_ref[0:own, LANES:]
    returns = [
        (rxp_ref, x_blocks(1)),
        (rxm_ref, x_blocks(-1)),
        (ryp_ref, y_blocks(1)),
        (rym_ref, y_blocks(-1)),
        (rzp_ref, z_blocks(1)),
        (rzm_ref, z_blocks(-1)),
    ]
    place = {}
    at = 2 * own
    for group in CLASSES:
        for off in group:
            place[off] = at
            at += plan.live(off)
    for (axis, sign), (ref, blocks) in zip(
        (("x", 1), ("x", -1), ("y", 1), ("y", -1), ("z", 1), ("z", -1)), returns
    ):
        row = 0
        for off in blocks:
            if plan.find(off)[:2] != (axis, sign):
                continue
            live = plan.live(off)
            if plan.rows(off) != live:
                ref[row : row + plan.rows(off), :] = jnp.zeros((plan.rows(off), 2 * LANES), F32)
            ref[row : row + live, :] = acc_ref[place[off] : place[off] + live, :]
            row += plan.rows(off)


def last_kernel(sel_ref, fg_ref, force_ref, wb_ref, *refs):
    returned = refs[:6]
    out_force_ref, out_fg_ref = refs[6:8]
    ret = jnp.concatenate([ref[...] for ref in returned], axis=0)
    sums = dot_tn(sel_ref[...], ret, HIGH)
    out_fg_ref[...] = fg_ref[...] + dot_nt(sums[:, 0:LANES], wb_ref[...], HIGH)
    total = (force_ref[...] + sums[:, LANES:]).T
    out_force_ref[...] = -(total[0:3, :] + total[3:6, :])


VMEM = pl.BlockSpec(memory_space=pltpu.VMEM)
SMEM = pl.BlockSpec(memory_space=pltpu.SMEM)
PARAMS = pltpu.CompilerParams(vmem_limit_bytes=52 * 2**20)


def shape(*dims, dtype=F32):
    return jax.ShapeDtypeStruct(dims, dtype)


def local(
    positions,
    atom_features,
    send_face,
    send_edge,
    send_corner,
    centre,
    other,
    edge_count,
    w_proj_a,
    w_proj_b,
    w_radial,
    w_first,
    w_env,
    w_value,
    w_second,
    w_out,
):
    own, chans = atom_features.shape
    edges = centre.shape[0]
    n_basis = w_radial.shape[0]
    plan = Plan([send_face.shape[2], send_edge.shape[2], send_corner.shape[2]])
    sizes = {axis: lax.axis_size(axis) for axis in AXES}
    wide = 2 * LANES
    n_ghost = sum(len(c) * w for c, w in zip(CLASSES, plan.widths))
    n_sel = 2 * own + n_ghost
    n_send = sum(plan.total(blocks) for blocks in SEND_GROUPS)

    dead = (own - 1) * (OTHER_MASK + 1) + OTHER_MASK
    key = jnp.where(
        jnp.arange(edges) < edge_count[0], centre * (OTHER_MASK + 1) + other, dead
    ).astype(jnp.int32)
    key = lax.sort(key, is_stable=False)
    edges_up = -(-edges // CHUNK) * CHUNK
    if edges_up != edges:
        key = jnp.concatenate([key, jnp.full((edges_up - edges,), dead, jnp.int32)])
    key = key.reshape(edges_up // LANES, LANES)

    with jax.named_scope("prep"):
        pa, pb, sel, *sends = pl.pallas_call(
            lambda *refs: prep_kernel(plan, *refs),
            out_shape=[shape(own, chans), shape(own, wide), shape(n_send, own)]
            + [shape(plan.total(blocks), wide) for blocks in SEND_GROUPS],
            in_specs=[VMEM] * 4 + [SMEM] * 3,
            out_specs=[VMEM] * 9,
            compiler_params=PARAMS,
        )(positions, atom_features, w_proj_a, w_proj_b, send_face, send_edge, send_corner)

    with jax.named_scope("halo"):
        got = {}
        got["z", 1], got["z", -1] = swap(sends[0], sends[1], "gz", sizes["gz"])

        def gather_message(own_part, blocks, axis):
            return jnp.concatenate(
                [own_part] + [plan.piece(got, off, axis) for off in blocks], axis=0
            )

        got["y", 1], got["y", -1] = swap(
            gather_message(sends[2], y_blocks(1)[3:], "y"),
            gather_message(sends[3], y_blocks(-1)[3:], "y"),
            "gy",
            sizes["gy"],
        )
        got["x", 1], got["x", -1] = swap(
            gather_message(sends[4], x_blocks(1)[1:], "x"),
            gather_message(sends[5], x_blocks(-1)[1:], "x"),
            "gx",
            sizes["gx"],
        )

    held = {}
    for axis, blocks in (("x", x_blocks), ("y", y_blocks), ("z", z_blocks)):
        for sign in (1, -1):
            held[axis, sign] = [
                off for off in blocks(sign) if plan.find(off)[:2] == (axis, sign)
            ]
    order = (("x", 1), ("x", -1), ("y", 1), ("y", -1), ("z", 1), ("z", -1))
    n_rows = edges_up // LANES
    n_chunks = edges_up // CHUNK
    n_table = n_sel + 4 * n_basis
    planes = (n_chunks, chans, CHUNK)
    scratch = [
        pltpu.VMEM((max(n_table, own + 4 * LANES), wide), F32),
        pltpu.VMEM((chans, n_table), BF16),
        pltpu.VMEM((chans, chans), BF16),
        pltpu.VMEM((2 * chans, chans), BF16),
        pltpu.VMEM((chans, 2 * chans), BF16),
        pltpu.VMEM((chans, 2 * chans), BF16),
        pltpu.VMEM((2 * n_basis, chans), BF16),
        pltpu.VMEM((chans, LANES), F32),
        pltpu.VMEM((n_rows * 8, LANES), F32),
        pltpu.VMEM((n_rows * n_basis, LANES), F32),
        pltpu.VMEM((8, n_rows, LANES), F32),
        pltpu.VMEM(planes, BF16),
        pltpu.VMEM(planes, BF16),
        pltpu.VMEM(planes, BF16),
        pltpu.VMEM(planes, BF16),
        pltpu.VMEM((edges_up // SUB, 9 * WIN, SUB), BF16),
        pltpu.VMEM((9, own + WIN, chans), F32),
        pltpu.VMEM((9, own + WIN, chans), F32),
        pltpu.VMEM((chans, CHUNK), F32),
        pltpu.VMEM(planes, BF16),
        pltpu.VMEM(planes, BF16),
        pltpu.VMEM(planes, BF16),
        pltpu.VMEM((n_chunks, CHUNK // LANES, LANES), F32),
        pltpu.VMEM((own + WIN, LANES), F32),
        pltpu.VMEM((10, CHUNK // LANES, LANES), F32),
        pltpu.VMEM((CHUNK // LANES * n_basis, LANES), F32),
        pltpu.VMEM((CHUNK // LANES * 16, LANES), F32),
        pltpu.VMEM((n_sel, wide), F32),
    ]
    with jax.named_scope("layer"):
        energy, fg, force, *back = pl.pallas_call(
            lambda *refs: main_kernel(plan, *refs),
            out_shape=[shape(1, own), shape(own, chans), shape(own, LANES)]
            + [shape(plan.total(held[side]), wide) for side in order],
            in_specs=[SMEM, SMEM] + [VMEM] * 17,
            out_specs=[VMEM] * 9,
            scratch_shapes=scratch,
            compiler_params=PARAMS,
        )(
            edge_count,
            key,
            key,
            pa,
            pb,
            got["z", 1],
            got["z", -1],
            got["y", 1],
            got["y", -1],
            got["x", 1],
            got["x", -1],
            w_proj_a,
            w_proj_b,
            w_radial,
            w_first,
            w_env,
            w_value,
            w_second,
            w_out.reshape(1, -1),
        )

    with jax.named_scope("halo_back"):
        mine = dict(zip(order, back))
        home = {}

        def put(blocks, parts, sign):
            at = 0
            for off in blocks:
                home[off] = lax.slice_in_dim(parts, at, at + plan.rows(off), axis=0)
                at += plan.rows(off)

        def message(axis, sign, blocks):
            pieces = []
            at = 0
            for off in blocks:
                if off in held[axis, sign]:
                    pieces.append(
                        lax.slice_in_dim(mine[axis, sign], at, at + plan.rows(off), axis=0)
                    )
                    at += plan.rows(off)
                else:
                    pieces.append(home[off])
            return jnp.concatenate(pieces, axis=0)

        for axis, name, blocks in (
            ("x", "gx", x_blocks),
            ("y", "gy", y_blocks),
            ("z", "gz", z_blocks),
        ):
            plus = message(axis, 1, blocks(1))
            minus = message(axis, -1, blocks(-1))
            plus, minus = swap(plus, minus, name, sizes[name], back=True)
            put(blocks(1), plus, 1)
            put(blocks(-1), minus, -1)
        returned = [
            jnp.concatenate([home[off] for off in blocks], axis=0) for blocks in SEND_GROUPS
        ]

    with jax.named_scope("owner_sums"):
        forces, feature_grad = pl.pallas_call(
            last_kernel,
            out_shape=[shape(3, own), shape(own, chans)],
            in_specs=[VMEM] * 10,
            out_specs=[VMEM] * 2,
            compiler_params=PARAMS,
        )(sel, fg, force, w_proj_b, *returned)
    return forces, energy.reshape(own), feature_grad


def solution(mesh):
    shard = P(AXES)
    return jax.shard_map(
        local,
        mesh=mesh,
        in_specs=(
            P(None, AXES),
            P(AXES, None),
            P(AXES, None, None),
            P(AXES, None, None),
            P(AXES, None, None),
            shard,
            shard,
            shard,
        )
        + (P(),) * 8,
        out_specs=(P(None, AXES), shard, P(AXES, None)),
        check_vma=False,
    )
```

time: 1540 us -> 74.9 us (0.05)
  other arithmetic: 856 us -> 5.62 us
  local copies, waits for them, and re-layouts: 545 us -> 5.41 us
  matrix products: 48.4 us -> 0 us
  waiting for transfers between devices: 48.6 us -> 22.6 us
  Pallas kernels: 0 us -> 21.3 us
    scatter-add x25 -> x0, other arithmetic: 784 us -> none  [the longest x9 301 us: local_energy(): jax.ops.segment_sum(env_weight * comp[:, None], centre, num_segments=n_own)]
    gather x67 -> x0, local copies, waits for them, and re-layouts: 469 us -> none  [the longest x18 184 us: local_energy(): total = total + comp[:, None] * jnp.take(env_m, centre, axis=0)]
    dot_general x16 -> x0, matrix products: 48.4 us -> none  [the longest x2 17.5 us: local_energy(): value = jnp.dot(first, w_value, preferred_element_type=jnp.float32)]
    mul x18 -> x0, local copies, waits for them, and re-layouts: 47.5 us -> none  [the longest x8 21.2 us: local_energy(): env_weight * comp[:, None]]
    mul x8 -> x0, other arithmetic: 30.5 us -> none  [the longest x2 21.5 us: local_energy(): total = total + comp[:, None] * jnp.take(env_m, centre, axis=0)]
    ppermute x24 -> x10, waiting for transfers between devices: 48.6 us -> 22.6 us  [the longest x8 17.5 us: swap(): return (lax.ppermute(plus, axis, up), lax.ppermute(minus, axis, down))]
    pallas_call x0 -> x3, Pallas kernels: none -> 21.3 us  [the longest x1 18.3 us: local(): pl.pallas_call(lambda *refs: main_kernel(plan, *refs), out_shape=[shape(1...]
    reduce_sum x4 -> x0, other arithmetic: 19.6 us -> none  [the longest x1 10.6 us: local_energy(): env_weight * comp[:, None]]
  transfers between devices with their start and end apart: 24 -> 10, of which waited for: 12 -> 8; matrix products, arithmetic and copies ran while one was open for 9% -> 8% of each run, Pallas kernels for 0% -> 0%
where the time goes in v1:
time: 74.9 us; the launch traced here: 74.2 us
  waiting for transfers between devices  22.6 us (30%)
  Pallas kernels  21.3 us (28%)
  starting transfers between devices  17.7 us (24%)
  other arithmetic  5.62 us (8%)
  local copies, waits for them, and re-layouts  5.41 us (7%)
  between operations  1.61 us (2%)
    pallas_call x1, Pallas kernels, local(): pl.pallas_call(lambda *refs: main_kernel(plan, *refs), out_shape=[shape(1...  18.3 us
    ppermute x8, waiting for transfers between devices, swap(): return (lax.ppermute(plus, axis, up), lax.ppermute(minus, axis, down))  17.5 us
    ppermute x8, starting transfers between devices, swap(): return (lax.ppermute(plus, axis, up), lax.ppermute(minus, axis, down))  14.1 us
    sort x1, other arithmetic, local(): key = lax.sort(key, is_stable=False)  5.58 us
    unnamed x63, local copies, waits for them, and re-layouts  5.35 us
    ppermute x2, waiting for transfers between devices, swap(): both = lax.ppermute(jnp.concatenate([plus, minus], axis=0), axis, up)  5.11 us
    ppermute x2, starting transfers between devices, swap(): both = lax.ppermute(jnp.concatenate([plus, minus], axis=0), axis, up)  3.61 us
    pallas_call x1, Pallas kernels, local(): pl.pallas_call(lambda *refs: prep_kernel(plan, *refs), out_shape=[shape(o...  1.52 us
  transfers between devices with their start and end apart: 10, of which 8 were waited for; matrix products, arithmetic and copies ran while one was open for 8% of the time, Pallas kernels for 0%

profile of v1, /device:TPU:0, one launch (start us, length us, event | category | flops | bytes accessed | tf_op | source)
XLA Modules:
  0.0 74.2 jit_solution(9955257683480975123)
XLA Ops:
  0.6 0.0 copy-start.15
  0.6 0.7 copy.19.refs_4_
  1.3 0.0 copy-done.15
  1.3 0.0 copy-start.14
  1.3 0.1 copy.21.refs_6_
  1.4 0.6 copy-done.14
  2.0 0.0 copy-start.10
  2.0 0.1 copy.20.refs_5_
  2.1 0.6 copy-done.10
  2.7 0.8 %copy-done = f32[128,128]{1,0:T(8,128)S(1)} copy-done((f32[128,128]{1,0:T(8,128)S(1)}, f32[128,128]{1,0:T(8,128)}, u32[]{:S(2)}) %copy-start) | copy-done | bytes 65560
  3.5 0.8 %copy-done.2 = f32[128,128]{1,0:T(8,128)S(1)} copy-done((f32[128,128]{1,0:T(8,128)S(1)}, f32[128,128]{1,0:T(8,128)}, u32[]{:S(2)}) %copy-start.2) | copy-done | bytes 65560
  4.4 0.8 %copy-done.4 = f32[128,128]{1,0:T(8,128)S(1)} copy-done((f32[128,128]{1,0:T(8,128)S(1)}, f32[128,128]{1,0:T(8,128)}, u32[]{:S(2)}) %copy-start.4) | copy-done | bytes 65560
  5.2 1.5 %prep.1 = (f32[128,128]{1,0:T(8,128)S(1)}, f32[128,256]{1,0:T(8,128)S(1)}, f32[352,128]{1,0:T(8,128)S(1)}, f32[96,256]{1,0:T(8,128)S(1)}, f32[96,256]{1,0:T(8,12...) custom-call(f32[3,128]{1,0:T(4,128)S(1)} %copy-done.10, ...), custom_call_target="tpu_custom_call" | custom-call | tf_op jit(solution)/shard_map/prep/pallas_call | solution.py:698
  6.7 0.0 copy-start.12
  6.8 0.0 copy-start.13
  6.8 3.0 %collective-permute-start = (f32[192,256]{1,0:T(8,128)S(1)}, f32[192,256]{1,0:T(8,128)S(1)}, u32[]{:S(2)}, u32[]{:S(2)}) collective-permute-start(f32[192,256]{1,0:T(8,128)S(1)} %pad_maximum_fusion), channel_id=1, source_target_pairs={{0,1},{1,0},{2,3},{3,2},{4,5},{5,4},{6,7},{7,6},{8,9},{9,8},{10,11... | collective-permute-start | bytes 589832 | tf_op jit(solution)/shard_map/halo/ppermute | solution.py:132
  10.5 0.0 copy-done.12
  10.5 0.0 copy-done.13
  10.5 5.6 %sort.7 = s32[6144]{0:T(1024)S(1)} sort(s32[6144]{0:T(1024)S(1)} %add_select_fusion), dimensions={0}, to_apply=%region_0.1 | sort | flops 79872 | bytes 49152 | tf_op jit(solution)/shard_map/sort | solution.py:691
  16.1 0.0 collective-permute-done
  16.1 1.6 %collective-permute-start.1 = (f32[96,256]{1,0:T(8,128)S(1)}, f32[96,256]{1,0:T(8,128)S(1)}, u32[]{:S(2)}, u32[]{:S(2)}) collective-permute-start(f32[96,256]{1,0:T(8,128)S(1)} %pad_maximum_fusion.1), channel_id=1, source_target_pairs={{0,2},{2,4},{4,6},{6,0},{1,3},{3,5},{5,7},{7,1},{8,10},{10,12},{12... | collective-permute-start | bytes 294920 | tf_op jit(solution)/shard_map/halo/ppermute | solution.py:135
  17.8 2.3 %collective-permute-start.2 = (f32[96,256]{1,0:T(8,128)S(1)}, f32[96,256]{1,0:T(8,128)S(1)}, u32[]{:S(2)}, u32[]{:S(2)}) collective-permute-start(f32[96,256]{1,0:T(8,128)S(1)} %pad_maximum_fusion.2), channel_id=1, source_target_pairs={{2,0},{4,2},{6,4},{0,6},{3,1},{5,3},{7,5},{1,7},{10,8},{12,10},{14... | collective-permute-start | bytes 294920 | tf_op jit(solution)/shard_map/halo/ppermute | solution.py:135
  20.1 3.4 %collective-permute-done.1.refs_7_ = f32[96,256]{1,0:T(8,128)S(1)} collective-permute-done((f32[96,256]{1,0:T(8,128)S(1)}, f32[96,256]{1,0:T(8,128)S(1)}, u32[]{:S(2)}, u32[]{:S(2)}) %collective-permute-start.1) | collective-permute-done | bytes 98336 | tf_op jit(solution)/shard_map/halo/ppermute | solution.py:135
  23.5 0.4 collective-permute-done.2.refs_8_
  23.9 0.3 collective-permute-start.4
  24.2 0.3 collective-permute-start.3
  24.5 2.1 %collective-permute-done.4.refs_10_ = f32[96,256]{1,0:T(8,128)S(1)} collective-permute-done((f32[96,256]{1,0:T(8,128)S(1)}, f32[96,256]{1,0:T(8,128)S(1)}, u32[]{:S(2)}, u32[]{:S(2)}) %collective-permute-start.4) | collective-permute-done | bytes 98336 | tf_op jit(solution)/shard_map/halo/ppermute | solution.py:135
  26.6 2.5 %collective-permute-done.3.refs_9_ = f32[96,256]{1,0:T(8,128)S(1)} collective-permute-done((f32[96,256]{1,0:T(8,128)S(1)}, f32[96,256]{1,0:T(8,128)S(1)}, u32[]{:S(2)}, u32[]{:S(2)}) %collective-permute-start.3) | collective-permute-done | bytes 98336 | tf_op jit(solution)/shard_map/halo/ppermute | solution.py:135
  29.2 0.0 copy-done.1
  29.2 0.0 copy-done.3
  29.2 0.0 copy-done.5
  29.2 0.0 copy-done.6
  29.2 0.0 copy-done.7
  29.2 0.0 copy-done.8
  29.2 0.6 copy-done.9
  29.8 0.0 copy-done.11
  29.8 18.3 %layer.1 = (f32[1,128]{1,0:T(1,128)}, f32[128,128]{1,0:T(8,128)S(1)}, f32[128,128]{1,0:T(8,128)S(1)}, f32[96,256]{1,0:T(8,128)S(1)}, f32[96,256]{1,0:T(8,128)S(1...) custom-call(s32[1]{0:T(128)} %copy.63.refs_0_, ...), custom_call_target="tpu_custom_call" | custom-call | tf_op jit(solution)/shard_map/layer/pallas_call | solution.py:771
  48.2 1.9 %collective-permute-start.5 = (f32[96,256]{1,0:T(8,128)S(1)}, f32[96,256]{1,0:T(8,128)S(1)}, u32[]{:S(2)}, u32[]{:S(2)}) collective-permute-start(f32[96,256]{1,0:T(8,128)S(1)} %get-tuple-element.35), channel_id=1, source_target_pairs={{0,8},{8,16},{16,24},{24,0},{1,9},{9,17},{17,25},{25,1},{2,10},{10... | collective-permute-start | bytes 294920 | tf_op jit(solution)/shard_map/halo_back/ppermute | solution.py:135
  50.1 3.3 %collective-permute-start.6 = (f32[96,256]{1,0:T(8,128)S(1)}, f32[96,256]{1,0:T(8,128)S(1)}, u32[]{:S(2)}, u32[]{:S(2)}) collective-permute-start(f32[96,256]{1,0:T(8,128)S(1)} %get-tuple-element.36), channel_id=1, source_target_pairs={{8,0},{16,8},{24,16},{0,24},{9,1},{17,9},{25,17},{1,25},{10,2},{18... | collective-permute-start | bytes 294920 | tf_op jit(solution)/shard_map/halo_back/ppermute | solution.py:135
  53.4 2.6 %collective-permute-done.5 = f32[96,256]{1,0:T(8,128)S(1)} collective-permute-done((f32[96,256]{1,0:T(8,128)S(1)}, f32[96,256]{1,0:T(8,128)S(1)}, u32[]{:S(2)}, u32[]{:S(2)}) %collective-permute-start.5) | collective-permute-done | bytes 98336 | tf_op jit(solution)/shard_map/halo_back/ppermute | solution.py:135
  56.0 0.0 collective-permute-done.6
  56.1 4.4 %collective-permute-start.7 = (f32[96,256]{1,0:T(8,128)S(1)}, f32[96,256]{1,0:T(8,128)S(1)}, u32[]{:S(2)}, u32[]{:S(2)}) collective-permute-start(f32[96,256]{1,0:T(8,128)S(1)} %get-tuple-element.56), channel_id=1, source_target_pairs={{2,0},{4,2},{6,4},{0,6},{3,1},{5,3},{7,5},{1,7},{10,8},{12,10},{14... | collective-permute-start | bytes 294920 | tf_op jit(solution)/shard_map/halo_back/ppermute | solution.py:135
  60.5 0.0 collective-permute-start.8
  60.5 2.2 %collective-permute-done.7 = f32[96,256]{1,0:T(8,128)S(1)} collective-permute-done((f32[96,256]{1,0:T(8,128)S(1)}, f32[96,256]{1,0:T(8,128)S(1)}, u32[]{:S(2)}, u32[]{:S(2)}) %collective-permute-start.7) | collective-permute-done | bytes 98336 | tf_op jit(solution)/shard_map/halo_back/ppermute | solution.py:135
  62.7 4.2 %collective-permute-done.8 = f32[96,256]{1,0:T(8,128)S(1)} collective-permute-done((f32[96,256]{1,0:T(8,128)S(1)}, f32[96,256]{1,0:T(8,128)S(1)}, u32[]{:S(2)}, u32[]{:S(2)}) %collective-permute-start.8) | collective-permute-done | bytes 98336 | tf_op jit(solution)/shard_map/halo_back/ppermute | solution.py:135
  67.0 0.6 collective-permute-start.9
  67.6 5.1 %collective-permute-done.9 = f32[192,256]{1,0:T(8,128)S(1)} collective-permute-done((f32[192,256]{1,0:T(8,128)S(1)}, f32[192,256]{1,0:T(8,128)S(1)}, u32[]{:S(2)}, u32[]{:S(2)}) %collective-permute-start.9) | collective-permute-done | bytes 196640 | tf_op jit(solution)/shard_map/halo_back/ppermute | solution.py:132
  72.8 1.4 %owner_sums.1 = (f32[3,128]{1,0:T(4,128)}, f32[128,128]{1,0:T(8,128)}) custom-call(f32[352,128]{1,0:T(8,128)S(1)} %get-tuple-element.23.sel_ref, f32[128,128]{1,0:T(8,128)S(1)} %get-tuple-element.32.fg_ref, f32[128,128]{1,0:T(8,128)S(1)} %get-tuple-element.33.force_ref, f32[128,128]{1,0:T(8,128)S(1)} %copy-done.1, f32[96,256]{1,0:T(8,128)S(1)} %get-tuple-element.44.refs_0_, ...), custom_call_target="tpu_custom_call" | custom-call | tf_op jit(solution)/shard_map/owner_sums/pallas_call | solution.py:839
  (53 shorter events, 0.2 us)
Async XLA Ops:
  0.6 0.7 copy-start.15
  1.3 0.7 copy-start.14
  2.0 0.7 copy-start.10
  2.7 0.8 %copy-start = (f32[128,128]{1,0:T(8,128)S(1)}, f32[128,128]{1,0:T(8,128)}, u32[]{:S(2)}) copy-start(f32[128,128]{1,0:T(8,128)} %wb_ref.1) | copy-start | bytes 196612
  3.5 0.8 %copy-start.2 = (f32[128,128]{1,0:T(8,128)S(1)}, f32[128,128]{1,0:T(8,128)}, u32[]{:S(2)}) copy-start(f32[128,128]{1,0:T(8,128)} %refs_11_.1) | copy-start | bytes 196612
  4.4 0.8 %copy-start.4 = (f32[128,128]{1,0:T(8,128)S(1)}, f32[128,128]{1,0:T(8,128)}, u32[]{:S(2)}) copy-start(f32[128,128]{1,0:T(8,128)} %refs_1_.1) | copy-start | bytes 196612
  6.7 3.7 %copy-start.12 = (s32[6144]{0:T(1024)S(1)}, s32[6144]{0:T(1024)}, u32[]{:S(2)}) copy-start(s32[6144]{0:T(1024)} %param.22) | copy-start | bytes 73732
  6.8 3.7 %copy-start.13 = (s32[6144]{0:T(1024)S(1)}, s32[6144]{0:T(1024)}, u32[]{:S(2)}) copy-start(s32[6144]{0:T(1024)} %param.21) | copy-start | bytes 73732
  6.8 9.3 %collective-permute-start = (f32[192,256]{1,0:T(8,128)S(1)}, f32[192,256]{1,0:T(8,128)S(1)}, u32[]{:S(2)}, u32[]{:S(2)}) collective-permute-start(f32[192,256]{1,0:T(8,128)S(1)} %pad_maximum_fusion), channel_id=1, source_target_pairs={{0,1},{1,0},{2,3},{3,2},{4,5},{5,4},{6,7},{7,6},{8,9},{9,8},{10,11... | collective-permute-start | bytes 589832 | tf_op jit(solution)/shard_map/halo/ppermute | solution.py:132
  16.1 7.4 %collective-permute-start.1 = (f32[96,256]{1,0:T(8,128)S(1)}, f32[96,256]{1,0:T(8,128)S(1)}, u32[]{:S(2)}, u32[]{:S(2)}) collective-permute-start(f32[96,256]{1,0:T(8,128)S(1)} %pad_maximum_fusion.1), channel_id=1, source_target_pairs={{0,2},{2,4},{4,6},{6,0},{1,3},{3,5},{5,7},{7,1},{8,10},{10,12},{12... | collective-permute-start | bytes 294920 | tf_op jit(solution)/shard_map/halo/ppermute | solution.py:135
  17.8 6.1 %collective-permute-start.2 = (f32[96,256]{1,0:T(8,128)S(1)}, f32[96,256]{1,0:T(8,128)S(1)}, u32[]{:S(2)}, u32[]{:S(2)}) collective-permute-start(f32[96,256]{1,0:T(8,128)S(1)} %pad_maximum_fusion.2), channel_id=1, source_target_pairs={{2,0},{4,2},{6,4},{0,6},{3,1},{5,3},{7,5},{1,7},{10,8},{12,10},{14... | collective-permute-start | bytes 294920 | tf_op jit(solution)/shard_map/halo/ppermute | solution.py:135
  23.9 2.7 %collective-permute-start.4 = (f32[96,256]{1,0:T(8,128)S(1)}, f32[96,256]{1,0:T(8,128)S(1)}, u32[]{:S(2)}, u32[]{:S(2)}) collective-permute-start(f32[96,256]{1,0:T(8,128)S(1)} %get-tuple-element.45), channel_id=1, source_target_pairs={{8,0},{16,8},{24,16},{0,24},{9,1},{17,9},{25,17},{1,25},{10,2},{18... | collective-permute-start | bytes 294920 | tf_op jit(solution)/shard_map/halo/ppermute | solution.py:135
  24.2 4.9 %copy-start.1 = (f32[128,128]{1,0:T(8,128)S(1)}, f32[128,128]{1,0:T(8,128)}, u32[]{:S(2)}) copy-start(f32[128,128]{1,0:T(8,128)} %wb_ref.1) | copy-start | bytes 196612
  24.2 4.9 %copy-start.3 = (f32[128,128]{1,0:T(8,128)S(1)}, f32[128,128]{1,0:T(8,128)}, u32[]{:S(2)}) copy-start(f32[128,128]{1,0:T(8,128)} %refs_11_.1) | copy-start | bytes 196612
  24.2 5.0 %copy-start.5 = (bf16[256,128]{1,0:T(8,128)(2,1)S(1)}, bf16[256,128]{1,0:T(8,128)(2,1)}, u32[]{:S(2)}) copy-start(bf16[256,128]{1,0:T(8,128)(2,1)} %refs_17_.1) | copy-start | bytes 196612
  24.2 4.9 %collective-permute-start.3 = (f32[96,256]{1,0:T(8,128)S(1)}, f32[96,256]{1,0:T(8,128)S(1)}, u32[]{:S(2)}, u32[]{:S(2)}) collective-permute-start(f32[96,256]{1,0:T(8,128)S(1)} %get-tuple-element.46), channel_id=1, source_target_pairs={{0,8},{8,16},{16,24},{24,0},{1,9},{9,17},{17,25},{25,1},{2,10},{10... | collective-permute-start | bytes 294920 | tf_op jit(solution)/shard_map/halo/ppermute | solution.py:135
  24.5 4.7 %copy-start.6 = (bf16[128,128]{1,0:T(8,128)(2,1)S(1)}, bf16[128,128]{1,0:T(8,128)(2,1)}, u32[]{:S(2)}) copy-start(bf16[128,128]{1,0:T(8,128)(2,1)} %refs_14_.1) | copy-start | bytes 98308
  24.5 4.7 %copy-start.7 = (bf16[128,128]{1,0:T(8,128)(2,1)S(1)}, bf16[128,128]{1,0:T(8,128)(2,1)}, u32[]{:S(2)}) copy-start(bf16[128,128]{1,0:T(8,128)(2,1)} %refs_15_.1) | copy-start | bytes 98308
  24.5 4.7 %copy-start.8 = (bf16[128,128]{1,0:T(8,128)(2,1)S(1)}, bf16[128,128]{1,0:T(8,128)(2,1)}, u32[]{:S(2)}) copy-start(bf16[128,128]{1,0:T(8,128)(2,1)} %refs_16_.1) | copy-start | bytes 98308
  29.2 0.7 copy-start.9
  29.2 0.7 copy-start.11
  48.2 7.9 %collective-permute-start.5 = (f32[96,256]{1,0:T(8,128)S(1)}, f32[96,256]{1,0:T(8,128)S(1)}, u32[]{:S(2)}, u32[]{:S(2)}) collective-permute-start(f32[96,256]{1,0:T(8,128)S(1)} %get-tuple-element.35), channel_id=1, source_target_pairs={{0,8},{8,16},{16,24},{24,0},{1,9},{9,17},{17,25},{25,1},{2,10},{10... | collective-permute-start | bytes 294920 | tf_op jit(solution)/shard_map/halo_back/ppermute | solution.py:135
  50.1 6.0 %collective-permute-start.6 = (f32[96,256]{1,0:T(8,128)S(1)}, f32[96,256]{1,0:T(8,128)S(1)}, u32[]{:S(2)}, u32[]{:S(2)}) collective-permute-start(f32[96,256]{1,0:T(8,128)S(1)} %get-tuple-element.36), channel_id=1, source_target_pairs={{8,0},{16,8},{24,16},{0,24},{9,1},{17,9},{25,17},{1,25},{10,2},{18... | collective-permute-start | bytes 294920 | tf_op jit(solution)/shard_map/halo_back/ppermute | solution.py:135
  56.1 6.6 %collective-permute-start.7 = (f32[96,256]{1,0:T(8,128)S(1)}, f32[96,256]{1,0:T(8,128)S(1)}, u32[]{:S(2)}, u32[]{:S(2)}) collective-permute-start(f32[96,256]{1,0:T(8,128)S(1)} %get-tuple-element.56), channel_id=1, source_target_pairs={{2,0},{4,2},{6,4},{0,6},{3,1},{5,3},{7,5},{1,7},{10,8},{12,10},{14... | collective-permute-start | bytes 294920 | tf_op jit(solution)/shard_map/halo_back/ppermute | solution.py:135
  60.5 6.4 %collective-permute-start.8 = (f32[96,256]{1,0:T(8,128)S(1)}, f32[96,256]{1,0:T(8,128)S(1)}, u32[]{:S(2)}, u32[]{:S(2)}) collective-permute-start(f32[96,256]{1,0:T(8,128)S(1)} %get-tuple-element.55), channel_id=1, source_target_pairs={{0,2},{2,4},{4,6},{6,0},{1,3},{3,5},{5,7},{7,1},{8,10},{10,12},{12... | collective-permute-start | bytes 294920 | tf_op jit(solution)/shard_map/halo_back/ppermute | solution.py:135
  67.0 5.7 %collective-permute-start.9 = (f32[192,256]{1,0:T(8,128)S(1)}, f32[192,256]{1,0:T(8,128)S(1)}, u32[]{:S(2)}, u32[]{:S(2)}) collective-permute-start(f32[192,256]{1,0:T(8,128)S(1)} %constant_dynamic-update-slice_fusion.36), channel_id=1, source_target_pairs={{1,0},{0,1},{3,2},{2,3},{5,4},{4,5},{7,6},{6,7},{9,8},{8,9},{11,10... | collective-permute-start | bytes 589832 | tf_op jit(solution)/shard_map/halo_back/ppermute | solution.py:132

commit v2 on v1

--- a/solution.py
+++ b/solution.py
@@ -84,6 +84,16 @@
     return blocks + [(s, 0, 1), (s, 0, -1)]
 
 
+SIDES = (("x", 1), ("x", -1), ("y", 1), ("y", -1), ("z", 1), ("z", -1))
+BLOCKS = {"x": x_blocks, "y": y_blocks, "z": z_blocks}
+
+
+def held_blocks(side):
+    axis, sign = side
+    first = {"x": 0, "y": 1, "z": 2}[axis]
+    return [off for off in BLOCKS[axis](sign) if all(o == 0 for o in off[:first])]
+
+
 SEND_GROUPS = [z_blocks(1), z_blocks(-1), y_own(1), y_own(-1), x_own(1), x_own(-1)]
 
 
@@ -95,18 +105,19 @@
         return self.widths[kind(off)]
 
     def rows(self, off):
-        return -(-self.live(off) // 8) * 8
+        return self.live(off) + 1
 
     def total(self, blocks):
         return sum(self.rows(off) for off in blocks)
 
+    def spans(self, blocks):
+        at = 0
+        for off in blocks:
+            yield off, at
+            at += self.rows(off)
+
     def start(self, blocks, off):
-        at = 0
-        for other in blocks:
-            if other == off:
-                return at
-            at += self.rows(other)
-        raise KeyError(off)
+        return dict(self.spans(blocks))[off]
 
     def find(self, off):
         if off[0] != 0:
@@ -135,33 +146,101 @@
     return lax.ppermute(plus, axis, up), lax.ppermute(minus, axis, down)
 
 
-def prep_kernel(plan, pos_ref, feat_ref, wa_ref, wb_ref, face_ref, edge_ref, corner_ref, *outs):
+GROUP = 32
+
+
+def group_rows(count):
+    row = lax.broadcasted_iota(jnp.int32, (count, LANES), 0)
+    group = lax.broadcasted_iota(jnp.int32, (count, LANES), 1) // GROUP
+    return (row == group).astype(F32) * (group < 3).astype(F32)
+
+
+def diagonal(x):
+    row = lax.broadcasted_iota(jnp.int32, x.shape, 0)
+    lane = lax.broadcasted_iota(jnp.int32, x.shape, 1)
+    return jnp.where((lane & (GROUP - 1)) == row, x, 0.0)
+
+
+def spread(row, live):
+    return diagonal(jnp.broadcast_to(row, (live, LANES)))
+
+
+def prep_kernel(plan, *refs):
+    inputs, outs = refs[:7], refs[7:16]
+    held, sem = refs[16:23], refs[23]
+    copies = [
+        pltpu.make_async_copy(src, dst, sem.at[i])
+        for i, (src, dst) in enumerate(zip(inputs, held))
+    ]
+    for copy in copies:
+        copy.start()
+    for copy in copies:
+        copy.wait()
+    pos_ref, feat_ref, wa_ref, wb_ref, face_ref, edge_ref, corner_ref = held
     pa_ref, pb_ref, sel_ref = outs[:3]
     sends = outs[3:9]
     own = feat_ref.shape[0]
-    feat = feat_ref[...]
-    pa_ref[...] = dot_nn(feat, wa_ref[...], HIGH)
-    pb_ref[:, 0:LANES] = dot_nn(feat, wb_ref[...], HIGH)
-    pos = jnp.concatenate([pos_ref[...], jnp.zeros((LANES - 3, own), F32)], axis=0)
-    pb_ref[:, LANES:] = pos.T
     lists = (face_ref, edge_ref, corner_ref)
     lane = lax.broadcasted_iota(jnp.int32, (1, own), 1)
     sel_ref[...] = jnp.zeros_like(sel_ref)
     at = 0
     for blocks in SEND_GROUPS:
         for off in blocks:
-            ref = lists[kind(off)]
             key = CLASSES[kind(off)].index(off)
-            for j in range(plan.live(off)):
-                row = ref[0, key, j]
-                sel_ref[at + j : at + j + 1, :] = (lane == row).astype(F32)
+            live = plan.live(off)
+            column = lists[kind(off)][0, :, key : key + 1]
+            sel_ref[at : at + live, :] = (column == lane).astype(F32)
             at += plan.rows(off)
-    packed = dot_nn(sel_ref[...], pb_ref[...], HIGH)
+    feat = feat_ref[...]
+    pb = dot_nn(feat, wb_ref[...], HIGH)
+    pb_ref[...] = pb
+    pos = dot_tn(pos_ref[...], group_rows(3), HIGH)
+    sel = sel_ref[...]
+    rows = dot_nn(sel, pb, HIGH)
+    places = dot_nn(sel, pos, HIGH)
     at = 0
     for blocks, send in zip(SEND_GROUPS, sends):
-        rows = plan.total(blocks)
-        send[...] = packed[at : at + rows, :]
-        at += rows
+        count = plan.total(blocks)
+        send[...] = rows[at : at + count, :]
+        for off, begin in plan.spans(blocks):
+            live = plan.live(off)
+            block = places[at + begin : at + begin + live, :]
+            send[begin + live : begin + live + 1, :] = jnp.sum(
+                diagonal(block), axis=0, keepdims=True
+            )
+        at += count
+    pa_ref[...] = dot_nn(feat, wa_ref[...], HIGH)
+
+
+def weight_kernel(
+    wrad_ref,
+    w1_ref,
+    wenv_ref,
+    wval_ref,
+    w2_ref,
+    wout_ref,
+    w1t_ref,
+    wevt_ref,
+    w2t_ref,
+    wev_ref,
+    wradb_ref,
+    wcol_ref,
+):
+    chans = w1_ref.shape[0]
+
+    def flip(w):
+        return w.astype(F32).T.astype(BF16)
+
+    w1t_ref[...] = flip(w1_ref[...])
+    wevt_ref[0:chans, :] = flip(wenv_ref[...])
+    wevt_ref[chans:, :] = flip(wval_ref[...])
+    w2t_ref[:, 0:chans] = flip(w2_ref[0:chans, :])
+    w2t_ref[:, chans:] = flip(w2_ref[chans:, :])
+    wev_ref[:, 0:chans] = wenv_ref[...]
+    wev_ref[:, chans:] = wval_ref[...]
+    rad = wrad_ref[...]
+    wradb_ref[...] = jnp.concatenate([rad, jnp.zeros_like(rad)], axis=0).astype(BF16)
+    wcol_ref[...] = jnp.broadcast_to(wout_ref[...].astype(F32), (LANES, chans)).T
 
 
 def harmonics(ux, uy, uz):
@@ -234,8 +313,9 @@
 def main_kernel(plan, *refs):
     (
         count_ref,
-        skey_ref,
+        bound_ref,
         key_ref,
+        pos_ref,
         pa_ref,
         pb_ref,
         zp_ref,
@@ -244,17 +324,17 @@
         ym_ref,
         xp_ref,
         xm_ref,
-        wa_ref,
-        wb_ref,
         wrad_ref,
         w1_ref,
-        wenv_ref,
-        wval_ref,
         w2_ref,
-        wout_ref,
-        energy_ref,
-        fg_ref,
-        force_ref,
+        w1t_ref,
+        wevt_ref,
+        w2t_ref,
+        wev_ref,
+        wradb_ref,
+        wcol_ref,
+        ae_ref,
+        own_ref,
         rxp_ref,
         rxm_ref,
         ryp_ref,
@@ -262,13 +342,8 @@
         rzp_ref,
         rzm_ref,
         tab_ref,
+        place_ref,
         table_ref,
-        w1t_ref,
-        wevt_ref,
-        w2t_ref,
-        wev_ref,
-        wradb_ref,
-        wcol_ref,
         y_ref,
         basis_ref,
         geo_ref,
@@ -283,8 +358,7 @@
         dt_ref,
         dv_ref,
         dfa_ref,
-        dmix_env_ref,
-        ae_ref,
+        live_ref,
         dy_ref,
         db_ref,
         dr_ref,
@@ -308,37 +382,27 @@
     n_tab = own + n_ghost
     n_sel = own + n_tab
 
-    tab_ref[...] = jnp.zeros_like(tab_ref)
-    tab_ref[0:own, 0:chans] = pa_ref[...]
+    tab_ref[0:own, :] = pa_ref[...]
     tab_ref[own : 2 * own, :] = pb_ref[...]
+    place_ref[...] = jnp.zeros_like(place_ref)
     at = 2 * own
     for group in CLASSES:
         for off in group:
             axis, sign, begin = plan.find(off)
             live = plan.live(off)
-            tab_ref[at : at + live, :] = messages[axis, sign][begin : begin + live, :]
+            message = messages[axis, sign]
+            tab_ref[at : at + live, :] = message[begin : begin + live, :]
+            place_ref[at - 2 * own : at - 2 * own + live, :] = spread(
+                message[begin + live : begin + live + 1, :], live
+            )
             at += live
-    pos_t = tab_ref[own : own + 4 * LANES, LANES:].T
-    rad = wrad_ref[...]
-    rad_hi, rad_lo = split(rad)
-    pad_at = n_sel
-    tab_ref[pad_at : pad_at + n_basis, 0:chans] = rad_hi
-    tab_ref[pad_at + n_basis : pad_at + 2 * n_basis, 0:chans] = rad_hi
-    tab_ref[pad_at + 2 * n_basis : pad_at + 3 * n_basis, 0:chans] = rad_lo
-    table_ref[...] = tab_ref[0 : table_ref.shape[1], 0:chans].T.astype(BF16)
-
-    def flip(w):
-        return w.astype(F32).T.astype(BF16)
-
-    w1t_ref[...] = flip(w1_ref[...])
-    wevt_ref[0:chans, :] = flip(wenv_ref[...])
-    wevt_ref[chans:, :] = flip(wval_ref[...])
-    w2t_ref[:, 0:chans] = flip(w2_ref[0:chans, :])
-    w2t_ref[:, chans:] = flip(w2_ref[chans:, :])
-    wev_ref[:, 0:chans] = wenv_ref[...]
-    wev_ref[:, chans:] = wval_ref[...]
-    wradb_ref[...] = jnp.concatenate([rad, jnp.zeros_like(rad)], axis=0).astype(BF16)
-    wcol_ref[...] = jnp.broadcast_to(wout_ref[...].astype(F32), (chans, LANES)).T
+    ghost_pos = dot_nt(group_rows(8), place_ref[...], HIGH)
+    pos_t = jnp.concatenate([pos_ref[...], ghost_pos[0:3, :]], axis=1)
+    rad_hi, rad_lo = split(wrad_ref[...])
+    tab_ref[n_sel : n_sel + 4 * n_basis, :] = jnp.concatenate(
+        [rad_hi, rad_hi, rad_lo, jnp.zeros_like(rad_lo)], axis=0
+    )
+    table_ref[...] = tab_ref[...].T.astype(BF16)
 
     keys = key_ref[...]
     centre = keys >> OTHER_BITS
@@ -372,9 +436,8 @@
     n_chunks = lax.div(count_ref[0] + (CHUNK - 1), jnp.int32(CHUNK))
 
     def window(k, s):
-        row = k * per + s * sub_rows
-        low = skey_ref[row, 0] >> OTHER_BITS
-        high = skey_ref[row + sub_rows - 1, LANES - 1] >> OTHER_BITS
+        low = bound_ref[0, k * subs + s]
+        high = bound_ref[1, k * subs + s]
         start = pl.multiple_of((low >> 3) << 3, 8)
         more = lax.div(high - start, jnp.int32(WIN))
         return start, more
@@ -487,7 +550,7 @@
         dy_ref[9, :, :] = jnp.zeros((per, LANES), F32)
         live = ee * row_of(7, k)
         for j in range(per):
-            dmix_env_ref[k, j : j + 1, :] = live[:, j * LANES : (j + 1) * LANES]
+            live_ref[k, j : j + 1, :] = live[:, j * LANES : (j + 1) * LANES]
         energy = ee * envv
         dz2 = ((wcol * envv) * (sg + second * (1.0 - sg))).astype(BF16)
         dj = dot_nn(w2_ref[...], dz2)
@@ -573,7 +636,7 @@
         denvelope = -(q * envelope) * dist
         dg = (denvelope - g) * inv
         sins, coss = waves(0.5 * dist, n_basis)
-        denv_direct = dmix_env_ref[k] + dy_ref[0] / envelope
+        denv_direct = live_ref[k] + dy_ref[0] / envelope
         ddist = denv_direct * denvelope
         for n in range(n_basis):
             db = db_ref[pl.ds(n, per, stride=n_basis), :]
@@ -604,50 +667,60 @@
 
     lax.fori_loop(0, n_chunks, phase_c, 0)
 
-    energy_ref[...] = jnp.sum(ae_ref[0:own, :].T, axis=0, keepdims=True)
-    fg_ref[...] = dot_nt(acc_ref[0:own, 0:chans], wa_ref[...], HIGH) + dot_nt(
-        acc_ref[own : 2 * own, 0:chans], wb_ref[...], HIGH
-    )
-    force_ref[...] = acc_ref[own : 2 * own, LANES:] - acc_ref[0:own, LANES:]
-    returns = [
-        (rxp_ref, x_blocks(1)),
-        (rxm_ref, x_blocks(-1)),
-        (ryp_ref, y_blocks(1)),
-        (rym_ref, y_blocks(-1)),
-        (rzp_ref, z_blocks(1)),
-        (rzm_ref, z_blocks(-1)),
-    ]
-    place = {}
+    own_ref[...] = acc_ref[0 : 2 * own, :]
+    row = lax.broadcasted_iota(jnp.int32, (LANES, LANES), 0)
+    group = lax.broadcasted_iota(jnp.int32, (LANES, LANES), 1) // GROUP
+    both = ((group < 3) & ((row == group) | (row == group + 3))).astype(F32)
+    places = dot_nn(acc_ref[2 * own :, LANES:], both, HIGH)
+    found = {}
     at = 2 * own
     for group in CLASSES:
         for off in group:
-            place[off] = at
+            found[off] = at
             at += plan.live(off)
-    for (axis, sign), (ref, blocks) in zip(
-        (("x", 1), ("x", -1), ("y", 1), ("y", -1), ("z", 1), ("z", -1)), returns
-    ):
-        row = 0
-        for off in blocks:
-            if plan.find(off)[:2] != (axis, sign):
-                continue
+    for side, ref in zip(SIDES, (rxp_ref, rxm_ref, ryp_ref, rym_ref, rzp_ref, rzm_ref)):
+        for off, row in plan.spans(held_blocks(side)):
             live = plan.live(off)
-            if plan.rows(off) != live:
-                ref[row : row + plan.rows(off), :] = jnp.zeros((plan.rows(off), 2 * LANES), F32)
-            ref[row : row + live, :] = acc_ref[place[off] : place[off] + live, :]
-            row += plan.rows(off)
-
-
-def last_kernel(sel_ref, fg_ref, force_ref, wb_ref, *refs):
+            at = found[off]
+            ref[row : row + live, :] = acc_ref[at : at + live, 0:chans]
+            block = places[at - 2 * own : at - 2 * own + live, :]
+            ref[row + live : row + live + 1, :] = jnp.sum(diagonal(block), axis=0, keepdims=True)
+
+
+def own_kernel(ae_ref, own_ref, wa_ref, wb_ref, energy_ref, fg_ref, force_ref):
+    chans = wa_ref.shape[1]
+    own = force_ref.shape[1]
+    energy_ref[...] = jnp.sum(ae_ref[0:own, :].T, axis=0, keepdims=True)
+    fg_ref[...] = dot_nt(own_ref[0:own, 0:chans], wa_ref[...], HIGH) + dot_nt(
+        own_ref[own:, 0:chans], wb_ref[...], HIGH
+    )
+    force = (own_ref[own:, LANES:] - own_ref[0:own, LANES:]).T
+    force_ref[...] = force[0:3, :] + force[3:6, :]
+
+
+def last_kernel(plan, sel_ref, fg_ref, force_ref, wb_ref, *refs):
     returned = refs[:6]
-    out_force_ref, out_fg_ref = refs[6:8]
+    out_force_ref, out_fg_ref, place_ref = refs[6:9]
     ret = jnp.concatenate([ref[...] for ref in returned], axis=0)
-    sums = dot_tn(sel_ref[...], ret, HIGH)
-    out_fg_ref[...] = fg_ref[...] + dot_nt(sums[:, 0:LANES], wb_ref[...], HIGH)
-    total = (force_ref[...] + sums[:, LANES:]).T
-    out_force_ref[...] = -(total[0:3, :] + total[3:6, :])
+    place_ref[...] = jnp.zeros_like(place_ref)
+    at = 0
+    for blocks, ref in zip(SEND_GROUPS, returned):
+        for off, row in plan.spans(blocks):
+            live = plan.live(off)
+            place_ref[at + row : at + row + live, :] = spread(
+                ref[row + live : row + live + 1, :], live
+            )
+        at += plan.total(blocks)
+    sel = sel_ref[...]
+    sums = dot_tn(sel, ret, HIGH)
+    places = dot_tn(sel, place_ref[...], HIGH)
+    out_fg_ref[...] = fg_ref[...] + dot_nt(sums, wb_ref[...], HIGH)
+    total = dot_nt(group_rows(8), places, HIGH)
+    out_force_ref[...] = -(force_ref[...] + total[0:3, :])
 
 
 VMEM = pl.BlockSpec(memory_space=pltpu.VMEM)
+HBM = pl.BlockSpec(memory_space=pltpu.HBM)
 SMEM = pl.BlockSpec(memory_space=pltpu.SMEM)
 PARAMS = pltpu.CompilerParams(vmem_limit_bytes=52 * 2**20)
 
@@ -679,10 +752,10 @@
     n_basis = w_radial.shape[0]
     plan = Plan([send_face.shape[2], send_edge.shape[2], send_corner.shape[2]])
     sizes = {axis: lax.axis_size(axis) for axis in AXES}
-    wide = 2 * LANES
     n_ghost = sum(len(c) * w for c, w in zip(CLASSES, plan.widths))
     n_sel = 2 * own + n_ghost
     n_send = sum(plan.total(blocks) for blocks in SEND_GROUPS)
+    n_table = n_sel + 4 * n_basis
 
     dead = (own - 1) * (OTHER_MASK + 1) + OTHER_MASK
     key = jnp.where(
@@ -692,17 +765,40 @@
     edges_up = -(-edges // CHUNK) * CHUNK
     if edges_up != edges:
         key = jnp.concatenate([key, jnp.full((edges_up - edges,), dead, jnp.int32)])
+    windows = (key >> OTHER_BITS).reshape(edges_up // SUB, SUB)
+    bounds = jnp.stack([windows[:, 0], windows[:, SUB - 1]])
     key = key.reshape(edges_up // LANES, LANES)
 
     with jax.named_scope("prep"):
+        given = (positions, atom_features, w_proj_a, w_proj_b) + tuple(
+            jnp.transpose(lists, (0, 2, 1)) for lists in (send_face, send_edge, send_corner)
+        )
         pa, pb, sel, *sends = pl.pallas_call(
             lambda *refs: prep_kernel(plan, *refs),
-            out_shape=[shape(own, chans), shape(own, wide), shape(n_send, own)]
-            + [shape(plan.total(blocks), wide) for blocks in SEND_GROUPS],
-            in_specs=[VMEM] * 4 + [SMEM] * 3,
+            out_shape=[shape(own, chans), shape(own, chans), shape(n_send, own)]
+            + [shape(plan.total(blocks), chans) for blocks in SEND_GROUPS],
+            in_specs=[HBM] * len(given),
             out_specs=[VMEM] * 9,
+            scratch_shapes=[pltpu.VMEM(x.shape, x.dtype) for x in given]
+            + [pltpu.SemaphoreType.DMA((len(given),))],
             compiler_params=PARAMS,
-        )(positions, atom_features, w_proj_a, w_proj_b, send_face, send_edge, send_corner)
+        )(*given)
+
+    with jax.named_scope("weights"):
+        weights = pl.pallas_call(
+            weight_kernel,
+            out_shape=[
+                shape(chans, chans, dtype=BF16),
+                shape(2 * chans, chans, dtype=BF16),
+                shape(chans, 2 * chans, dtype=BF16),
+                shape(chans, 2 * chans, dtype=BF16),
+                shape(2 * n_basis, chans, dtype=BF16),
+                shape(chans, LANES),
+            ],
+            in_specs=[VMEM] * 6,
+            out_specs=[VMEM] * 6,
+            compiler_params=PARAMS,
+        )(w_radial, w_first, w_env, w_value, w_second, w_out.reshape(1, -1))
 
     with jax.named_scope("halo"):
         got = {}
@@ -726,26 +822,13 @@
             sizes["gx"],
         )
 
-    held = {}
-    for axis, blocks in (("x", x_blocks), ("y", y_blocks), ("z", z_blocks)):
-        for sign in (1, -1):
-            held[axis, sign] = [
-                off for off in blocks(sign) if plan.find(off)[:2] == (axis, sign)
-            ]
-    order = (("x", 1), ("x", -1), ("y", 1), ("y", -1), ("z", 1), ("z", -1))
     n_rows = edges_up // LANES
     n_chunks = edges_up // CHUNK
-    n_table = n_sel + 4 * n_basis
     planes = (n_chunks, chans, CHUNK)
     scratch = [
-        pltpu.VMEM((max(n_table, own + 4 * LANES), wide), F32),
+        pltpu.VMEM((n_table, chans), F32),
+        pltpu.VMEM((-(-n_ghost // LANES) * LANES, LANES), F32),
         pltpu.VMEM((chans, n_table), BF16),
-        pltpu.VMEM((chans, chans), BF16),
-        pltpu.VMEM((2 * chans, chans), BF16),
-        pltpu.VMEM((chans, 2 * chans), BF16),
-        pltpu.VMEM((chans, 2 * chans), BF16),
-        pltpu.VMEM((2 * n_basis, chans), BF16),
-        pltpu.VMEM((chans, LANES), F32),
         pltpu.VMEM((n_rows * 8, LANES), F32),
         pltpu.VMEM((n_rows * n_basis, LANES), F32),
         pltpu.VMEM((8, n_rows, LANES), F32),
@@ -761,25 +844,25 @@
         pltpu.VMEM(planes, BF16),
         pltpu.VMEM(planes, BF16),
         pltpu.VMEM((n_chunks, CHUNK // LANES, LANES), F32),
-        pltpu.VMEM((own + WIN, LANES), F32),
         pltpu.VMEM((10, CHUNK // LANES, LANES), F32),
         pltpu.VMEM((CHUNK // LANES * n_basis, LANES), F32),
         pltpu.VMEM((CHUNK // LANES * 16, LANES), F32),
-        pltpu.VMEM((n_sel, wide), F32),
+        pltpu.VMEM((n_sel, 2 * LANES), F32),
     ]
     with jax.named_scope("layer"):
-        energy, fg, force, *back = pl.pallas_call(
+        atom_sums, own_sums, *back = pl.pallas_call(
             lambda *refs: main_kernel(plan, *refs),
-            out_shape=[shape(1, own), shape(own, chans), shape(own, LANES)]
-            + [shape(plan.total(held[side]), wide) for side in order],
-            in_specs=[SMEM, SMEM] + [VMEM] * 17,
-            out_specs=[VMEM] * 9,
+            out_shape=[shape(own + WIN, LANES), shape(2 * own, 2 * LANES)]
+            + [shape(plan.total(held_blocks(side)), chans) for side in SIDES],
+            in_specs=[SMEM, SMEM] + [VMEM] * 19,
+            out_specs=[VMEM] * 8,
             scratch_shapes=scratch,
             compiler_params=PARAMS,
         )(
             edge_count,
+            bounds,
             key,
-            key,
+            positions,
             pa,
             pb,
             got["z", 1],
@@ -788,59 +871,55 @@
             got["y", -1],
             got["x", 1],
             got["x", -1],
-            w_proj_a,
-            w_proj_b,
             w_radial,
             w_first,
-            w_env,
-            w_value,
             w_second,
-            w_out.reshape(1, -1),
+            *weights,
         )
 
+    with jax.named_scope("own_part"):
+        energy, fg, force = pl.pallas_call(
+            own_kernel,
+            out_shape=[shape(1, own), shape(own, chans), shape(3, own)],
+            in_specs=[VMEM] * 4,
+            out_specs=[VMEM] * 3,
+            compiler_params=PARAMS,
+        )(atom_sums, own_sums, w_proj_a, w_proj_b)
+
     with jax.named_scope("halo_back"):
-        mine = dict(zip(order, back))
+        mine = dict(zip(SIDES, back))
         home = {}
 
-        def put(blocks, parts, sign):
-            at = 0
-            for off in blocks:
-                home[off] = lax.slice_in_dim(parts, at, at + plan.rows(off), axis=0)
-                at += plan.rows(off)
-
-        def message(axis, sign, blocks):
+        def message(side):
+            at = dict(plan.spans(held_blocks(side)))
             pieces = []
-            at = 0
-            for off in blocks:
-                if off in held[axis, sign]:
+            for off in BLOCKS[side[0]](side[1]):
+                if off in at:
+                    begin = at[off]
                     pieces.append(
-                        lax.slice_in_dim(mine[axis, sign], at, at + plan.rows(off), axis=0)
+                        lax.slice_in_dim(mine[side], begin, begin + plan.rows(off), axis=0)
                     )
-                    at += plan.rows(off)
                 else:
                     pieces.append(home[off])
             return jnp.concatenate(pieces, axis=0)
 
-        for axis, name, blocks in (
-            ("x", "gx", x_blocks),
-            ("y", "gy", y_blocks),
-            ("z", "gz", z_blocks),
-        ):
-            plus = message(axis, 1, blocks(1))
-            minus = message(axis, -1, blocks(-1))
-            plus, minus = swap(plus, minus, name, sizes[name], back=True)
-            put(blocks(1), plus, 1)
-            put(blocks(-1), minus, -1)
+        for axis, name in (("x", "gx"), ("y", "gy"), ("z", "gz")):
+            sides = ((axis, 1), (axis, -1))
+            pair = swap(*(message(side) for side in sides), name, sizes[name], back=True)
+            for (_, sign), got_back in zip(sides, pair):
+                for off, at in plan.spans(BLOCKS[axis](sign)):
+                    home[off] = lax.slice_in_dim(got_back, at, at + plan.rows(off), axis=0)
         returned = [
             jnp.concatenate([home[off] for off in blocks], axis=0) for blocks in SEND_GROUPS
         ]
 
     with jax.named_scope("owner_sums"):
         forces, feature_grad = pl.pallas_call(
-            last_kernel,
+            lambda *refs: last_kernel(plan, *refs),
             out_shape=[shape(3, own), shape(own, chans)],
             in_specs=[VMEM] * 10,
             out_specs=[VMEM] * 2,
+            scratch_shapes=[pltpu.VMEM((n_send, LANES), F32)],
             compiler_params=PARAMS,
         )(sel, fg, force, w_proj_b, *returned)
     return forces, energy.reshape(own), feature_grad

time: 74.9 us -> 66.2 us (0.88)
  waiting for transfers between devices: 22.6 us -> 11 us
  starting transfers between devices: 17.7 us -> 20 us
  local copies, waits for them, and re-layouts: 5.41 us -> 7.5 us
  Pallas kernels: 21.3 us -> 20.2 us
    ppermute x8, waiting for transfers between devices: 17.5 us -> 9.09 us  [swap(): return (lax.ppermute(plus, axis, up), lax.ppermute(minus, axis, down))]
    ppermute x2, waiting for transfers between devices: 5.11 us -> 1.86 us  [swap(): both = lax.ppermute(jnp.concatenate([plus, minus], axis=0), axis, up)]
    ppermute x2, starting transfers between devices: 3.61 us -> 5.61 us  [swap(): both = lax.ppermute(jnp.concatenate([plus, minus], axis=0), axis, up)]
    concatenate x1 -> x2, local copies, waits for them, and re-layouts: 0.01 us -> 1.32 us  [message(): return jnp.concatenate(pieces, axis=0)]
    unnamed x63 -> x33, local copies, waits for them, and re-layouts: 5.35 us -> 4.67 us
    pallas_call x2 -> x4, Pallas kernels: 19.8 us -> 19.1 us  [the longest x1 16.8 us: local(): pl.pallas_call(lambda *refs: main_kernel(plan, *refs), out_shape=[shape(o...]
  transfers between devices with their start and end apart: 10 -> 10, of which waited for: 8 -> 8; matrix products, arithmetic and copies ran while one was open for 8% -> 10% of each run, Pallas kernels for 0% -> 1%
where the time goes in v2:
time: 66.2 us; the launch traced here: 65.9 us
  Pallas kernels  20.2 us (31%)
  starting transfers between devices  20 us (30%)
  waiting for transfers between devices  11 us (17%)
  local copies, waits for them, and re-layouts  7.5 us (11%)
  other arithmetic  5.63 us (9%)
  between operations  1.62 us (2%)
    pallas_call x1, Pallas kernels, local(): pl.pallas_call(lambda *refs: main_kernel(plan, *refs), out_shape=[shape(o...  16.8 us
    ppermute x8, starting transfers between devices, swap(): return (lax.ppermute(plus, axis, up), lax.ppermute(minus, axis, down))  14.4 us
    ppermute x8, waiting for transfers between devices, swap(): return (lax.ppermute(plus, axis, up), lax.ppermute(minus, axis, down))  9.09 us
    ppermute x2, starting transfers between devices, swap(): both = lax.ppermute(jnp.concatenate([plus, minus], axis=0), axis, up)  5.61 us
    sort x1, other arithmetic, local(): key = lax.sort(key, is_stable=False)  5.58 us
    unnamed x33, local copies, waits for them, and re-layouts  4.67 us
    ppermute x2, waiting for transfers between devices, swap(): both = lax.ppermute(jnp.concatenate([plus, minus], axis=0), axis, up)  1.86 us
    pallas_call x1, Pallas kernels, local(): pl.pallas_call(lambda *refs: last_kernel(plan, *refs), out_shape=[shape(3...  1.41 us
  transfers between devices with their start and end apart: 10, of which 8 were waited for; matrix products, arithmetic and copies ran while one was open for 10% of the time, Pallas kernels for 1%

profile of v2, /device:TPU:0, one launch (start us, length us, event | category | flops | bytes accessed | tf_op | source)
XLA Modules:
  0.0 65.9 jit_solution(14140871098486145845)
XLA Ops:
  0.6 0.0 copy-start.11
  0.6 0.8 %copy.21 = s32[1,6,32]{1,2,0:T(8,128)S(1)} copy(s32[1,6,32]{2,0,1:T(1,128)} %param.18) | data formatting | bytes 1536 | tf_op args[2]
  1.4 0.7 %copy-done.10 = f32[3,128]{1,0:T(4,128)S(1)} copy-done((f32[3,128]{1,0:T(4,128)S(1)}, f32[3,128]{1,0:T(4,128)}, u32[]{:S(2)}) %copy-start.10) | copy-done | bytes 1560
  2.1 0.0 copy-done.12
  2.1 0.8 %copy-done = f32[128,128]{1,0:T(8,128)S(1)} copy-done((f32[128,128]{1,0:T(8,128)S(1)}, f32[128,128]{1,0:T(8,128)}, u32[]{:S(2)}) %copy-start) | copy-done | bytes 65560
  2.9 0.8 %copy-done.2 = f32[128,128]{1,0:T(8,128)S(1)} copy-done((f32[128,128]{1,0:T(8,128)S(1)}, f32[128,128]{1,0:T(8,128)}, u32[]{:S(2)}) %copy-start.2) | copy-done | bytes 65560
  3.8 0.8 %copy-done.6 = f32[128,128]{1,0:T(8,128)S(1)} copy-done((f32[128,128]{1,0:T(8,128)S(1)}, f32[128,128]{1,0:T(8,128)}, u32[]{:S(2)}) %copy-start.6) | copy-done | bytes 65560
  4.6 1.1 %prep.1 = (f32[128,128]{1,0:T(8,128)S(1)}, f32[128,128]{1,0:T(8,128)S(1)}, f32[330,128]{1,0:T(8,128)S(1)}, f32[81,128]{1,0:T(8,128)S(1)}, f32[81,128]{1,0:T(8,12...) custom-call(f32[3,128]{1,0:T(4,128)S(1)} %copy-done.10, ...), custom_call_target="tpu_custom_call" | custom-call | tf_op jit(solution)/shard_map/prep/pallas_call | solution.py:776
  5.7 0.0 copy-start.14
  5.7 0.0 copy-start.15
  5.7 3.0 %collective-permute-start = (f32[162,128]{1,0:T(8,128)S(1)}, f32[162,128]{1,0:T(8,128)S(1)}, u32[]{:S(2)}, u32[]{:S(2)}) collective-permute-start(f32[162,128]{1,0:T(8,128)S(1)} %pad_maximum_fusion), channel_id=1, source_target_pairs={{0,1},{1,0},{2,3},{3,2},{4,5},{5,4},{6,7},{7,6},{8,9},{9,8},{10,11... | collective-permute-start | bytes 248840 | tf_op jit(solution)/shard_map/halo/ppermute | solution.py:143
  9.4 0.0 copy-start.7
  9.4 0.0 copy-start.8
  9.5 5.6 %sort.7 = s32[6144]{0:T(1024)S(1)} sort(s32[6144]{0:T(1024)S(1)} %add_select_fusion), dimensions={0}, to_apply=%region_0.1 | sort | flops 79872 | bytes 49152 | tf_op jit(solution)/shard_map/sort | solution.py:764
  15.1 0.0 copy-start.5
  15.1 0.0 copy-start.9
  15.1 0.2 slice_reduce_fusion.1
  15.3 0.0 copy-start.13
  15.3 0.6 copy-done.4
  15.9 0.1 copy-done.13
  15.9 0.1 weights.1
  16.1 0.0 collective-permute-done
  16.2 1.6 %collective-permute-start.1 = (f32[81,128]{1,0:T(8,128)S(1)}, f32[81,128]{1,0:T(8,128)S(1)}, u32[]{:S(2)}, u32[]{:S(2)}) collective-permute-start(f32[81,128]{1,0:T(8,128)S(1)} %pad_maximum_fusion.1), channel_id=1, source_target_pairs={{0,2},{2,4},{4,6},{6,0},{1,3},{3,5},{5,7},{7,1},{8,10},{10,12},{12... | collective-permute-start | bytes 124424 | tf_op jit(solution)/shard_map/halo/ppermute | solution.py:146
  17.8 2.3 %collective-permute-start.2 = (f32[81,128]{1,0:T(8,128)S(1)}, f32[81,128]{1,0:T(8,128)S(1)}, u32[]{:S(2)}, u32[]{:S(2)}) collective-permute-start(f32[81,128]{1,0:T(8,128)S(1)} %pad_maximum_fusion.2), channel_id=1, source_target_pairs={{2,0},{4,2},{6,4},{0,6},{3,1},{5,3},{7,5},{1,7},{10,8},{12,10},{14... | collective-permute-start | bytes 124424 | tf_op jit(solution)/shard_map/halo/ppermute | solution.py:146
  20.1 2.3 %collective-permute-done.1.refs_8_ = f32[81,128]{1,0:T(8,128)S(1)} collective-permute-done((f32[81,128]{1,0:T(8,128)S(1)}, f32[81,128]{1,0:T(8,128)S(1)}, u32[]{:S(2)}, u32[]{:S(2)}) %collective-permute-start.1) | collective-permute-done | bytes 41504 | tf_op jit(solution)/shard_map/halo/ppermute | solution.py:146
  22.4 0.0 collective-permute-done.2.refs_9_
  22.4 0.2 concatenate.39
  22.7 0.1 collective-permute-start.4
  22.7 0.2 concatenate.38
  23.0 0.5 collective-permute-start.3
  23.5 0.9 %collective-permute-done.4.refs_11_ = f32[81,128]{1,0:T(8,128)S(1)} collective-permute-done((f32[81,128]{1,0:T(8,128)S(1)}, f32[81,128]{1,0:T(8,128)S(1)}, u32[]{:S(2)}, u32[]{:S(2)}) %collective-permute-start.4) | collective-permute-done | bytes 41504 | tf_op jit(solution)/shard_map/halo/ppermute | solution.py:146
  24.4 2.3 %collective-permute-done.3.refs_10_ = f32[81,128]{1,0:T(8,128)S(1)} collective-permute-done((f32[81,128]{1,0:T(8,128)S(1)}, f32[81,128]{1,0:T(8,128)S(1)}, u32[]{:S(2)}, u32[]{:S(2)}) %collective-permute-start.3) | collective-permute-done | bytes 41504 | tf_op jit(solution)/shard_map/halo/ppermute | solution.py:146
  26.7 16.8 %layer.1 = (f32[144,128]{1,0:T(8,128)S(1)}, f32[256,256]{1,0:T(8,128)S(1)}, f32[81,128]{1,0:T(8,128)S(1)}, f32[81,128]{1,0:T(8,128)S(1)}, f32[51,128]{1,0:T(8,12...) custom-call(s32[1]{0:T(128)} %copy.22.refs_0_, s32[2,24]{1,0:T(2,128)S(1)} %pad_add_fusion.refs_1_, ...), custom_call_target="tpu_custom_call" | custom-call | tf_op jit(solution)/shard_map/layer/pallas_call | solution.py:853
  43.5 0.1 collective-permute-start.5
  43.6 5.9 %collective-permute-start.6 = (f32[81,128]{1,0:T(8,128)S(1)}, f32[81,128]{1,0:T(8,128)S(1)}, u32[]{:S(2)}, u32[]{:S(2)}) collective-permute-start(f32[81,128]{1,0:T(8,128)S(1)} %get-tuple-element.52), channel_id=1, source_target_pairs={{8,0},{16,8},{24,16},{0,24},{9,1},{17,9},{25,17},{1,25},{10,2},{18... | collective-permute-start | bytes 124424 | tf_op jit(solution)/shard_map/halo_back/ppermute | solution.py:146
  49.5 1.6 %collective-permute-done.5 = f32[81,128]{1,0:T(8,128)S(1)} collective-permute-done((f32[81,128]{1,0:T(8,128)S(1)}, f32[81,128]{1,0:T(8,128)S(1)}, u32[]{:S(2)}, u32[]{:S(2)}) %collective-permute-start.5) | collective-permute-done | bytes 41504 | tf_op jit(solution)/shard_map/halo_back/ppermute | solution.py:146
  51.1 0.1 collective-permute-done.6
  51.2 0.7 %concatenate.41 = f32[81,128]{1,0:T(8,128)S(1)} concatenate(f32[33,128]{1,0:T(8,128)S(1)} %slice.306, f32[9,128]{1,0:T(8,128)S(1)} %get-tuple-element.79, f32[9,128]{1,0:T(8,128)S(1)} %get-tuple-element.75, f32[9,128]{1,0:T(8,128)S(1)} %get-tuple-element.106, f32[3,128]{1,0:T(4,128)S(1)} %get-tuple-element.90, f32[3,128]{1,0:T(4,128)S(1)} %get-tuple-element.86, ...), dimensions={0} | concatenate | bytes 82944 | tf_op jit(solution)/shard_map/halo_back/concatenate | solution.py:904
  51.9 1.4 %collective-permute-start.8 = (f32[81,128]{1,0:T(8,128)S(1)}, f32[81,128]{1,0:T(8,128)S(1)}, u32[]{:S(2)}, u32[]{:S(2)}) collective-permute-start(f32[81,128]{1,0:T(8,128)S(1)} %concatenate.41), channel_id=1, source_target_pairs={{0,2},{2,4},{4,6},{6,0},{1,3},{3,5},{5,7},{7,1},{8,10},{10,12},{12... | collective-permute-start | bytes 124424 | tf_op jit(solution)/shard_map/halo_back/ppermute | solution.py:146
  53.3 0.7 concatenate.40
  54.0 2.5 %collective-permute-start.7 = (f32[81,128]{1,0:T(8,128)S(1)}, f32[81,128]{1,0:T(8,128)S(1)}, u32[]{:S(2)}, u32[]{:S(2)}) collective-permute-start(f32[81,128]{1,0:T(8,128)S(1)} %concatenate.40), channel_id=1, source_target_pairs={{2,0},{4,2},{6,4},{0,6},{3,1},{5,3},{7,5},{1,7},{10,8},{12,10},{14... | collective-permute-start | bytes 124424 | tf_op jit(solution)/shard_map/halo_back/ppermute | solution.py:146
  56.5 1.3 %collective-permute-done.8 = f32[81,128]{1,0:T(8,128)S(1)} collective-permute-done((f32[81,128]{1,0:T(8,128)S(1)}, f32[81,128]{1,0:T(8,128)S(1)}, u32[]{:S(2)}, u32[]{:S(2)}) %collective-permute-start.8) | collective-permute-done | bytes 41504 | tf_op jit(solution)/shard_map/halo_back/ppermute | solution.py:146
  57.8 0.6 collective-permute-done.7
  58.4 0.7 %concatenate.42 = f32[162,128]{1,0:T(8,128)S(1)} concatenate(f32[15,128]{1,0:T(8,128)S(1)} %get-tuple-element.84, f32[15,128]{1,0:T(8,128)S(1)} %get-tuple-element.82, f32[33,128]{1,0:T(8,128)S(1)} %get-tuple-element.54, f32[9,128]{1,0:T(8,128)S(1)} %get-tuple-element.78, f32[9,128]{1,0:T(8,128)S(1)} %get-tuple-element.74, f32[15,128]{1,0:T(8,128)S(1)} %get-tuple-element.83, ...), dimensions={0} | concatenate | bytes 165888 | tf_op jit(solution)/shard_map/halo_back/concatenate | solution.py:143
  59.1 2.6 %collective-permute-start.9 = (f32[162,128]{1,0:T(8,128)S(1)}, f32[162,128]{1,0:T(8,128)S(1)}, u32[]{:S(2)}, u32[]{:S(2)}) collective-permute-start(f32[162,128]{1,0:T(8,128)S(1)} %concatenate.42), channel_id=1, source_target_pairs={{1,0},{0,1},{3,2},{2,3},{5,4},{4,5},{7,6},{6,7},{9,8},{8,9},{11,10... | collective-permute-start | bytes 248840 | tf_op jit(solution)/shard_map/halo_back/ppermute | solution.py:143
  61.7 0.8 %own_part.1 = (f32[1,128]{1,0:T(1,128)}, f32[128,128]{1,0:T(8,128)S(1)}, f32[3,128]{1,0:T(4,128)S(1)}) custom-call(f32[144,128]{1,0:T(8,128)S(1)} %get-tuple-element.46.ae_ref, f32[256,256]{1,0:T(8,128)S(1)} %get-tuple-element.47.own_ref, f32[128,128]{1,0:T(8,128)S(1)} %copy-done.3, f32[128,128]{1,0:T(8,128)S(1)} %copy-done.1), custom_call_target="tpu_custom_call" | custom-call | tf_op jit(solution)/shard_map/own_part/pallas_call | solution.py:881
  62.6 1.9 %collective-permute-done.9 = f32[162,128]{1,0:T(8,128)S(1)} collective-permute-done((f32[162,128]{1,0:T(8,128)S(1)}, f32[162,128]{1,0:T(8,128)S(1)}, u32[]{:S(2)}, u32[]{:S(2)}) %collective-permute-start.9) | collective-permute-done | bytes 82976 | tf_op jit(solution)/shard_map/halo_back/ppermute | solution.py:143
  64.5 1.4 %owner_sums.1 = (f32[3,128]{1,0:T(4,128)}, f32[128,128]{1,0:T(8,128)}) custom-call(f32[330,128]{1,0:T(8,128)S(1)} %get-tuple-element.31.refs_0_, f32[128,128]{1,0:T(8,128)S(1)} %get-tuple-element.48.refs_1_, f32[3,128]{1,0:T(4,128)S(1)} %get-tuple-element.49.refs_2_, f32[128,128]{1,0:T(8,128)S(1)} %copy-done.1, f32[81,128]{1,0:T(8,128)S(1)} %get-tuple-element.62.refs_4_, ...), custom_call_target="tpu_custom_call" | custom-call | tf_op jit(solution)/shard_map/owner_sums/pallas_call | solution.py:917
  (46 shorter events, 0.2 us)
Async XLA Ops:
  0.6 0.8 %copy-start.11 = (s32[1,12,8]{1,2,0:T(8,128)S(1)}, s32[1,12,8]{1,2,0:T(8,128)}, u32[]{:S(2)}) copy-start(s32[1,12,8]{1,2,0:T(8,128)} %param.19) | copy-start | bytes 1156
  1.4 0.7 %copy-start.10 = (f32[3,128]{1,0:T(4,128)S(1)}, f32[3,128]{1,0:T(4,128)}, u32[]{:S(2)}) copy-start(f32[3,128]{1,0:T(4,128)} %refs_3_.4) | copy-start | bytes 4612
  1.4 0.7 %copy-start.12 = (s32[1,8,2]{1,2,0:T(2,128)S(1)}, s32[1,8,2]{1,2,0:T(2,128)}, u32[]{:S(2)}) copy-start(s32[1,8,2]{1,2,0:T(2,128)} %param.20) | copy-start | bytes 196
  2.1 0.8 %copy-start = (f32[128,128]{1,0:T(8,128)S(1)}, f32[128,128]{1,0:T(8,128)}, u32[]{:S(2)}) copy-start(f32[128,128]{1,0:T(8,128)} %refs_3_.5) | copy-start | bytes 196612
  2.9 0.8 %copy-start.2 = (f32[128,128]{1,0:T(8,128)S(1)}, f32[128,128]{1,0:T(8,128)}, u32[]{:S(2)}) copy-start(f32[128,128]{1,0:T(8,128)} %wa_ref.1) | copy-start | bytes 196612
  3.8 0.8 %copy-start.6 = (f32[128,128]{1,0:T(8,128)S(1)}, f32[128,128]{1,0:T(8,128)}, u32[]{:S(2)}) copy-start(f32[128,128]{1,0:T(8,128)} %refs_1_.1) | copy-start | bytes 196612
  5.7 3.7 %copy-start.14 = (s32[6144]{0:T(1024)S(1)}, s32[6144]{0:T(1024)}, u32[]{:S(2)}) copy-start(s32[6144]{0:T(1024)} %param.22) | copy-start | bytes 73732
  5.7 3.7 %copy-start.15 = (s32[6144]{0:T(1024)S(1)}, s32[6144]{0:T(1024)}, u32[]{:S(2)}) copy-start(s32[6144]{0:T(1024)} %param.21) | copy-start | bytes 73732
  5.7 10.4 %collective-permute-start = (f32[162,128]{1,0:T(8,128)S(1)}, f32[162,128]{1,0:T(8,128)S(1)}, u32[]{:S(2)}, u32[]{:S(2)}) collective-permute-start(f32[162,128]{1,0:T(8,128)S(1)} %pad_maximum_fusion), channel_id=1, source_target_pairs={{0,1},{1,0},{2,3},{3,2},{4,5},{5,4},{6,7},{7,6},{8,9},{9,8},{10,11... | collective-permute-start | bytes 248840 | tf_op jit(solution)/shard_map/halo/ppermute | solution.py:143
  9.4 5.9 %copy-start.7 = (bf16[128,128]{1,0:T(8,128)(2,1)S(1)}, bf16[128,128]{1,0:T(8,128)(2,1)}, u32[]{:S(2)}) copy-start(bf16[128,128]{1,0:T(8,128)(2,1)} %wenv_ref.1) | copy-start | bytes 98308
  9.4 5.9 %copy-start.8 = (bf16[128,128]{1,0:T(8,128)(2,1)S(1)}, bf16[128,128]{1,0:T(8,128)(2,1)}, u32[]{:S(2)}) copy-start(bf16[128,128]{1,0:T(8,128)(2,1)} %wval_ref.1) | copy-start | bytes 98308
  15.0 0.8 %copy-start.4 = (bf16[256,128]{1,0:T(8,128)(2,1)S(1)}, bf16[256,128]{1,0:T(8,128)(2,1)}, u32[]{:S(2)}) copy-start(bf16[256,128]{1,0:T(8,128)(2,1)} %refs_14_.1) | copy-start | bytes 196612
  15.1 0.8 %copy-start.5 = (bf16[128,128]{1,0:T(8,128)(2,1)S(1)}, bf16[128,128]{1,0:T(8,128)(2,1)}, u32[]{:S(2)}) copy-start(bf16[128,128]{1,0:T(8,128)(2,1)} %refs_13_.1) | copy-start | bytes 98308
  15.1 0.8 %copy-start.9 = (f32[8,128]{1,0:T(8,128)S(1)}, f32[8,128]{1,0:T(8,128)}, u32[]{:S(2)}) copy-start(f32[8,128]{1,0:T(8,128)} %refs_12_.1) | copy-start | bytes 12292
  15.3 0.7 %copy-start.13 = (bf16[128]{0:T(256)(128)(2,1)S(1)}, bf16[128]{0:T(256)(128)(2,1)}, u32[]{:S(2)}) copy-start(bf16[128]{0:T(256)(128)(2,1)} %param.31) | copy-start | bytes 772
  16.2 6.2 %collective-permute-start.1 = (f32[81,128]{1,0:T(8,128)S(1)}, f32[81,128]{1,0:T(8,128)S(1)}, u32[]{:S(2)}, u32[]{:S(2)}) collective-permute-start(f32[81,128]{1,0:T(8,128)S(1)} %pad_maximum_fusion.1), channel_id=1, source_target_pairs={{0,2},{2,4},{4,6},{6,0},{1,3},{3,5},{5,7},{7,1},{8,10},{10,12},{12... | collective-permute-start | bytes 124424 | tf_op jit(solution)/shard_map/halo/ppermute | solution.py:146
  17.8 4.6 %collective-permute-start.2 = (f32[81,128]{1,0:T(8,128)S(1)}, f32[81,128]{1,0:T(8,128)S(1)}, u32[]{:S(2)}, u32[]{:S(2)}) collective-permute-start(f32[81,128]{1,0:T(8,128)S(1)} %pad_maximum_fusion.2), channel_id=1, source_target_pairs={{2,0},{4,2},{6,4},{0,6},{3,1},{5,3},{7,5},{1,7},{10,8},{12,10},{14... | collective-permute-start | bytes 124424 | tf_op jit(solution)/shard_map/halo/ppermute | solution.py:146
  22.7 1.8 %collective-permute-start.4 = (f32[81,128]{1,0:T(8,128)S(1)}, f32[81,128]{1,0:T(8,128)S(1)}, u32[]{:S(2)}, u32[]{:S(2)}) collective-permute-start(f32[81,128]{1,0:T(8,128)S(1)} %concatenate.39), channel_id=1, source_target_pairs={{8,0},{16,8},{24,16},{0,24},{9,1},{17,9},{25,17},{1,25},{10,2},{18... | collective-permute-start | bytes 124424 | tf_op jit(solution)/shard_map/halo/ppermute | solution.py:146
  23.0 3.8 %collective-permute-start.3 = (f32[81,128]{1,0:T(8,128)S(1)}, f32[81,128]{1,0:T(8,128)S(1)}, u32[]{:S(2)}, u32[]{:S(2)}) collective-permute-start(f32[81,128]{1,0:T(8,128)S(1)} %concatenate.38), channel_id=1, source_target_pairs={{0,8},{8,16},{16,24},{24,0},{1,9},{9,17},{17,25},{25,1},{2,10},{10... | collective-permute-start | bytes 124424 | tf_op jit(solution)/shard_map/halo/ppermute | solution.py:146
  43.5 7.6 %collective-permute-start.5 = (f32[81,128]{1,0:T(8,128)S(1)}, f32[81,128]{1,0:T(8,128)S(1)}, u32[]{:S(2)}, u32[]{:S(2)}) collective-permute-start(f32[81,128]{1,0:T(8,128)S(1)} %get-tuple-element.51), channel_id=1, source_target_pairs={{0,8},{8,16},{16,24},{24,0},{1,9},{9,17},{17,25},{25,1},{2,10},{10... | collective-permute-start | bytes 124424 | tf_op jit(solution)/shard_map/halo_back/ppermute | solution.py:146
  43.6 7.6 %collective-permute-start.6 = (f32[81,128]{1,0:T(8,128)S(1)}, f32[81,128]{1,0:T(8,128)S(1)}, u32[]{:S(2)}, u32[]{:S(2)}) collective-permute-start(f32[81,128]{1,0:T(8,128)S(1)} %get-tuple-element.52), channel_id=1, source_target_pairs={{8,0},{16,8},{24,16},{0,24},{9,1},{17,9},{25,17},{1,25},{10,2},{18... | collective-permute-start | bytes 124424 | tf_op jit(solution)/shard_map/halo_back/ppermute | solution.py:146
  51.9 5.9 %collective-permute-start.8 = (f32[81,128]{1,0:T(8,128)S(1)}, f32[81,128]{1,0:T(8,128)S(1)}, u32[]{:S(2)}, u32[]{:S(2)}) collective-permute-start(f32[81,128]{1,0:T(8,128)S(1)} %concatenate.41), channel_id=1, source_target_pairs={{0,2},{2,4},{4,6},{6,0},{1,3},{3,5},{5,7},{7,1},{8,10},{10,12},{12... | collective-permute-start | bytes 124424 | tf_op jit(solution)/shard_map/halo_back/ppermute | solution.py:146
  54.0 4.4 %collective-permute-start.7 = (f32[81,128]{1,0:T(8,128)S(1)}, f32[81,128]{1,0:T(8,128)S(1)}, u32[]{:S(2)}, u32[]{:S(2)}) collective-permute-start(f32[81,128]{1,0:T(8,128)S(1)} %concatenate.40), channel_id=1, source_target_pairs={{2,0},{4,2},{6,4},{0,6},{3,1},{5,3},{7,5},{1,7},{10,8},{12,10},{14... | collective-permute-start | bytes 124424 | tf_op jit(solution)/shard_map/halo_back/ppermute | solution.py:146
  58.4 3.3 %copy-start.1 = (f32[128,128]{1,0:T(8,128)S(1)}, f32[128,128]{1,0:T(8,128)}, u32[]{:S(2)}) copy-start(f32[128,128]{1,0:T(8,128)} %refs_3_.5) | copy-start | bytes 196612
  58.4 3.3 %copy-start.3 = (f32[128,128]{1,0:T(8,128)S(1)}, f32[128,128]{1,0:T(8,128)}, u32[]{:S(2)}) copy-start(f32[128,128]{1,0:T(8,128)} %wa_ref.1) | copy-start | bytes 196612
  59.1 5.3 %collective-permute-start.9 = (f32[162,128]{1,0:T(8,128)S(1)}, f32[162,128]{1,0:T(8,128)S(1)}, u32[]{:S(2)}, u32[]{:S(2)}) collective-permute-start(f32[162,128]{1,0:T(8,128)S(1)} %concatenate.42), channel_id=1, source_target_pairs={{1,0},{0,1},{3,2},{2,3},{5,4},{4,5},{7,6},{6,7},{9,8},{8,9},{11,10... | collective-permute-start | bytes 248840 | tf_op jit(solution)/shard_map/halo_back/ppermute | solution.py:143
